TPU v7x, 512 devices: a whole 4x4x16 slice. The times are simulated.
512 devices in a mesh: fsdp: 64 (over z, x), tp: 8 (over y, core).
Axes of the slice: x: 4, y: 4, z: 16, core: 2. Of those that a mesh axis runs over, the one named last changes fastest.
Arguments:
- momentum: float32 [8192, 14336], P('fsdp', 'tp'), may hold values from -45 to 45, as said below
- gradient: bfloat16 [8192, 14336], P('fsdp', 'tp'), may hold values from -6 to 6
- right_basis: float32 [14336, 512], P(('tp', 'fsdp')), may hold values from -0.046875 to 0.046875
Outputs:
- new_momentum: float32 [8192, 14336], P('fsdp', 'tp')
- new_basis: float32 [14336, 512], P(('tp', 'fsdp'))
- update: bfloat16 [8192, 14336], P('fsdp', 'tp')
Inputs may be any that keep to these rules, and one draw needn't show every extreme that they name: Entries of momentum have magnitudes that vary by row and by column.
All inputs are finite; a program needn't handle non-finite values.
Results may differ from a plain program's by a relative error of at most 0.001.
Values sent between devices are 32-bit elements; how exact they have to be, the bound alone decides.
A program may use at most 64 MiB of HBM per device.

v0:
```python
import jax
import jax.numpy as jnp
from jax import lax
from jax.sharding import PartitionSpec as P

ROWS = 8192
COLS = 14336
RANK = 512


def shards(momentum, gradient, right_basis):
    high = lax.Precision.HIGHEST
    blended = momentum + gradient.astype(jnp.float32)
    columns = blended
    partial_left = jnp.dot(
        columns,
        lax.all_gather(right_basis, "fsdp", axis=0, tiled=True),
        precision=high,
        preferred_element_type=jnp.float32,
    )
    left = lax.psum(partial_left, "tp")
    gram_local = jnp.dot(left.T, left, precision=high, preferred_element_type=jnp.float32)
    gram = lax.psum(gram_local, "fsdp")
    lower = jnp.linalg.cholesky(gram)
    ortho = jax.scipy.linalg.solve_triangular(lower, left.T, lower=True).T
    columns = blended
    right_part = lax.psum_scatter(
        jnp.dot(columns.T, ortho, precision=high, preferred_element_type=jnp.float32),
        "fsdp",
        scatter_dimension=0,
        tiled=True,
    )
    block = lax.all_gather(right_part, "fsdp", axis=0, tiled=True)
    squares = lax.psum(jnp.sum(right_part * right_part, axis=0), ("fsdp", "tp"))
    inverse = 1.0 / (jnp.sqrt(squares) + 1e-06)
    new_basis = right_part * inverse
    basis_block = block * inverse
    new_momentum = blended - 0.1 * jnp.dot(
        ortho, block.T, precision=high, preferred_element_type=jnp.float32
    )
    factor = jnp.sqrt(jnp.float32(ROWS) * jnp.float32(COLS) / jnp.float32(RANK))
    update = (
        factor * jnp.dot(ortho, basis_block.T, precision=high, preferred_element_type=jnp.float32)
    ).astype(jnp.bfloat16)
    return (new_momentum, new_basis, update)


def solution(mesh):
    placed = (P("fsdp", "tp"), P("fsdp", "tp"), P(("tp", "fsdp"), None))
    return jax.shard_map(
        shards,
        mesh=mesh,
        in_specs=placed,
        out_specs=(P("fsdp", "tp"), P(("tp", "fsdp"), None), P("fsdp", "tp")),
        check_vma=False,
    )
```

profile of v0, /device:TPU:1, one launch (start us, length us, event | category | flops | bytes accessed | tf_op | source)
XLA Modules:
  0.0 1136.0 jit_solution(5595436937965622078)
XLA Ops:
  8.0 146.7 %all-gather.5.cloned.1.call-done = f32[64,28,512]{2,1,0:T(8,128)} async-done(((f32[1,28,512]{2,1,0:T(8,128)}), f32[64,28,512]{2,1,0:T(8,128)}) %all-gather.5.cloned.1.call-update) | async-done | bytes 3670032 | tf_op jit(solution)/shard_map/all_gather | solution.py:17
  154.7 4.7 reshape.66
  159.5 4.9 fusion.13
  164.5 76.7 %all-reduce.6.cloned.1.call-done = f32[128,512]{1,0:T(8,128)} async-done(((f32[128,512]{1,0:T(8,128)}), f32[128,512]{1,0:T(8,128)}) %all-reduce.6.cloned.1.call-update) | async-done | bytes 262160 | tf_op jit(solution)/shard_map/psum | solution.py:21
  241.1 3.1 fusion.47
  244.5 264.2 %all-reduce.8.cloned.1.call-done = f32[512,512]{0,1:T(8,128)} async-done(((f32[512,512]{0,1:T(8,128)}), f32[512,512]{0,1:T(8,128)}) %all-reduce.8.cloned.1.call-update) | async-done | bytes 1048592 | tf_op jit(solution)/shard_map/psum | solution.py:23
  511.7 11.7 %cholesky.104 = f32[128,128]{1,0:T(8,128)S(1)} custom-call(f32[128,128]{1,0:T(8,128)S(1)} %cholesky.266), custom_call_target="Cholesky" | custom-call | tf_op jit(solution)/shard_map/jit(cholesky)/cholesky | solution.py:24
  523.5 10.4 custom-call.31
  536.8 12.5 %cholesky.217 = f32[128,128]{1,0:T(8,128)S(1)} custom-call(f32[128,128]{1,0:T(8,128)} %cholesky.270), custom_call_target="Cholesky" | custom-call | tf_op jit(solution)/shard_map/jit(cholesky)/cholesky | solution.py:24
  550.0 10.8 custom-call.32
  563.1 12.3 %cholesky.238 = f32[128,128]{1,0:T(8,128)} custom-call(f32[128,128]{1,0:T(8,128)S(1)} %cholesky.275), custom_call_target="Cholesky" | custom-call | tf_op jit(solution)/shard_map/jit(cholesky)/cholesky | solution.py:24
  577.0 10.4 custom-call.33
  588.9 11.7 %cholesky.255 = f32[128,128]{1,0:T(8,128)S(1)} custom-call(f32[128,128]{1,0:T(8,128)S(1)} %convolution_subtract_fusion.5), custom_call_target="Cholesky" | custom-call | tf_op jit(solution)/shard_map/jit(cholesky)/cholesky | solution.py:24
  605.1 10.5 while.1
  605.7 2.0 bitcast_dynamic-update-slice_fusion.2
  608.3 2.0 bitcast_dynamic-update-slice_fusion.2
  610.9 2.0 bitcast_dynamic-update-slice_fusion.2
  613.5 2.0 bitcast_dynamic-update-slice_fusion.2
  615.5 40.1 %custom-call.34 = f32[4,128,128]{1,2,0:T(8,128)S(1)} custom-call(f32[4,128,128]{2,1,0:T(8,128)} %get-tuple-element.10), custom_call_target="InvertDiagBlocksLowerTriangular" | custom-call | tf_op jit(solution)/shard_map/jit(_solve_triangular)/triangular_solve | solution.py:25
  661.4 4.9 fusion.12
  666.2 141.3 %fusion = f32[32,512]{1,0:T(8,128)S(1)} fusion(f32[1792,512]{1,0:T(8,128)} %fusion.12), kind=kCustom, calls=%all-reduce-scatter | all-reduce-scatter fusion | flops 1048577 | bytes 3737600
  810.2 4.2 collective-permute-start.7
  814.3 2.7 collective-permute-start.4
  817.1 5.0 collective-permute-start.3
  822.1 7.0 collective-permute-start.2
  829.1 3.2 collective-permute-start.1
  832.3 3.1 collective-permute-start
  838.6 142.8 %psum.23 = f32[512]{0:T(512)S(1)} all-reduce(f32[512]{0:T(512)S(1)} %multiply_reduce_fusion), channel_id=1, replica_groups=mesh['fsdp'=64,'tp'=8] {'fsdp','tp'}, use_global_device_ids=true, to_apply=%region_12.13 | all-reduce | flops 512 | bytes 4096 | tf_op jit(solution)/shard_map/psum | solution.py:34
  982.0 130.7 %all-gather.7.cloned.1.call-done = f32[64,28,512]{2,1,0:T(8,128)} async-done(((f32[1,28,512]{2,1,0:T(8,128)}), f32[64,28,512]{2,1,0:T(8,128)}) %all-gather.7.cloned.1.call-update) | async-done | bytes 3670032 | tf_op jit(solution)/shard_map/all_gather | solution.py:33
  1112.7 4.7 reshape.68
  1117.4 7.0 fusion.7
  1124.4 4.9 fusion.6
  (72 shorter events, 28.5 us)
Async XLA Ops:
  7.2 147.5 %all-gather.5.cloned.1.call-start = ((), (), s32[]{:S(2)}) async-start(), calls=%async_computation.2 | async-start | bytes 4259840 | tf_op jit(solution)/shard_map/all_gather | solution.py:17
  7.9 151.6 %copy-start.1 = (f32[128,1792]{1,0:T(8,128)S(1)}, f32[128,1792]{1,0:T(8,128)}, u32[]{:S(2)}) copy-start(f32[128,1792]{1,0:T(8,128)} %param.3) | copy-start | bytes 2752516
  7.9 151.5 %copy-start.2 = (bf16[128,1792]{1,0:T(8,128)(2,1)S(1)}, bf16[128,1792]{1,0:T(8,128)(2,1)}, u32[]{:S(2)}) copy-start(bf16[128,1792]{1,0:T(8,128)(2,1)} %param.4) | copy-start | bytes 1376260
  7.9 233.2 %all-reduce.6.cloned.1.call-start = ((), (), s32[]{:S(2)}) async-start(), calls=%async_computation | async-start | bytes 524288 | tf_op jit(solution)/shard_map/psum | solution.py:21
  164.4 344.3 %all-reduce.8.cloned.1.call-start = ((), (), s32[]{:S(2)}) async-start(), calls=%async_computation.1 | async-start | bytes 2097152 | tf_op jit(solution)/shard_map/psum | solution.py:23
  244.2 868.4 %all-gather.7.cloned.1.call-start = ((), (), s32[]{:S(2)}) async-start(), calls=%async_computation.3 | async-start | bytes 4259840 | tf_op jit(solution)/shard_map/all_gather | solution.py:33
  535.5 0.7 copy-start.3
  562.4 0.7 copy-start.4
  807.5 21.5 %collective-permute-start.6 = (f32[32,512]{1,0:T(8,128)S(1)}, f32[32,512]{1,0:T(8,128)S(1)}, u32[]{:S(2)}, u32[]{:S(2)}) collective-permute-start(f32[32,512]{1,0:T(8,128)S(1)} %fusion), channel_id=1, source_target_pairs={{0,56},{8,64},{16,72},{24,80},{32,88},{40,96},{48,104},{56,112},{6... | collective-permute-start | bytes 196616
  808.8 23.4 %collective-permute-start.5 = (f32[32,512]{1,0:T(8,128)S(1)}, f32[32,512]{1,0:T(8,128)S(1)}, u32[]{:S(2)}, u32[]{:S(2)}) collective-permute-start(f32[32,512]{1,0:T(8,128)S(1)} %fusion), channel_id=1, source_target_pairs={{0,48},{8,56},{16,64},{24,72},{32,80},{40,88},{48,96},{56,104},{64... | collective-permute-start | bytes 196616
  810.2 11.9 %collective-permute-start.7 = (f32[28,512]{1,0:T(8,128)S(1)}, f32[28,512]{1,0:T(8,128)S(1)}, u32[]{:S(2)}, u32[]{:S(2)}) collective-permute-start(f32[28,512]{1,0:T(8,128)S(1)} %slice.125), channel_id=1, source_target_pairs={{0,64},{8,72},{16,80},{24,88},{32,96},{40,104},{48,112},{56,120},{... | collective-permute-start | bytes 172040
  814.3 23.0 %collective-permute-start.4 = (f32[32,512]{1,0:T(8,128)S(1)}, f32[32,512]{1,0:T(8,128)S(1)}, u32[]{:S(2)}, u32[]{:S(2)}) collective-permute-start(f32[32,512]{1,0:T(8,128)S(1)} %fusion), channel_id=1, source_target_pairs={{0,40},{8,48},{16,56},{24,64},{32,72},{40,80},{48,88},{56,96},{64,... | collective-permute-start | bytes 196616
  817.1 20.2 %collective-permute-start.3 = (f32[32,512]{1,0:T(8,128)S(1)}, f32[32,512]{1,0:T(8,128)S(1)}, u32[]{:S(2)}, u32[]{:S(2)}) collective-permute-start(f32[32,512]{1,0:T(8,128)S(1)} %fusion), channel_id=1, source_target_pairs={{0,32},{8,40},{16,48},{24,56},{32,64},{40,72},{48,80},{56,88},{64,... | collective-permute-start | bytes 196616
  822.1 15.3 %collective-permute-start.2 = (f32[32,512]{1,0:T(8,128)S(1)}, f32[32,512]{1,0:T(8,128)S(1)}, u32[]{:S(2)}, u32[]{:S(2)}) collective-permute-start(f32[32,512]{1,0:T(8,128)S(1)} %fusion), channel_id=1, source_target_pairs={{0,24},{8,32},{16,40},{24,48},{32,56},{40,64},{48,72},{56,80},{64,... | collective-permute-start | bytes 196616
  829.1 8.3 collective-permute-start.1
  832.3 5.1 collective-permute-start
  1117.4 7.0 copy-start
Sparse Core Ops, SparseCore 0:
  10.9 143.7 all-gather.4
  164.5 76.5 all-reduce.5
  244.9 263.7 all-reduce.7
  982.1 130.4 all-gather.6
where the time goes:
time: 1150 us; the launch traced here: 1140 us
  waiting for transfers between devices  619 us (54%)
  blocking collectives  284 us (25%)
  other arithmetic  126 us (11%)
  matrix products  34.9 us (3%)
  starting transfers between devices  28.1 us (2%)
  local copies, waits for them, and re-layouts  26 us (2%)
  between operations  17.5 us (2%)
    psum x1, waiting for transfers between devices, shards(): gram = lax.psum(gram_local, 'fsdp')  264 us
    all_gather x1, waiting for transfers between devices, shards(): lax.all_gather(right_basis, 'fsdp', axis=0, tiled=True)  147 us
    psum x1, blocking collectives, shards(): squares = lax.psum(jnp.sum(right_part * right_part, axis=0), ('fsdp', 'tp'))  143 us
    unnamed x1, blocking collectives  141 us
    all_gather x1, waiting for transfers between devices, shards(): block = lax.all_gather(right_part, 'fsdp', axis=0, tiled=True)  131 us
    another operation x14, other arithmetic, shards(): lower = jnp.linalg.cholesky(gram)  83.6 us
    psum x1, waiting for transfers between devices, shards(): left = lax.psum(partial_left, 'tp')  76.7 us
    another operation x3, other arithmetic, shards(): ortho = jax.scipy.linalg.solve_triangular(lower, left.T, lower=True).T  40.6 us
  transfers between devices with their start and end apart: 12, of which 4 were waited for; matrix products, arithmetic and copies ran while one was open for 0% of the time, Pallas kernels for 0%

commit v1 on v0

v1 whole, which is shorter than its diff:
```python
import functools

import jax
import jax.numpy as jnp
from jax import lax
from jax.experimental import pallas as pl
from jax.experimental.pallas import tpu as pltpu
from jax.sharding import PartitionSpec as P

ROWS = 8192
COLS = 14336
RANK = 512
MESH = pl.DeviceIdType.MESH
LANE = 128
NX = 4
VMEM = pl.BlockSpec(memory_space=pltpu.VMEM)
F32 = jnp.float32
BF16 = jnp.bfloat16
NN = (((1,), (0,)), ((), ()))
TN = (((0,), (0,)), ((), ()))
NT = (((1,), (1,)), ((), ()))


def split2(v):
    hi = v.astype(BF16)
    return hi, (v - hi.astype(F32)).astype(BF16)


def dot3(a, b, dims):
    ah, al = a if isinstance(a, tuple) else split2(a)
    bh, bl = b if isinstance(b, tuple) else split2(b)
    d = functools.partial(lax.dot_general, dimension_numbers=dims, preferred_element_type=F32)
    return d(ah, bh) + (d(ah, bl) + d(al, bh))


def copy_to(src, dst, send, recv, where):
    return pltpu.make_async_remote_copy(
        src_ref=src, dst_ref=dst, send_sem=send, recv_sem=recv, device_id=where, device_id_type=MESH
    )


def greet(peers):
    barrier = pltpu.get_barrier_semaphore()
    for peer in peers:
        pl.semaphore_signal(barrier, inc=1, device_id=peer, device_id_type=MESH)
    pl.semaphore_wait(barrier, len(peers))


class Place:
    def __init__(self, nz):
        me = lax.axis_index("fsdp")
        self.nz = nz
        self.z = me // NX
        self.x = lax.rem(me, NX)

    def zat(self, d):
        return lax.rem(self.z + (d + self.nz), self.nz)

    def xat(self, d):
        return lax.rem(self.x + (d + NX), NX)

    def dev(self, dz, dx):
        return {"fsdp": self.zat(dz) * NX + self.xat(dx)}

    def ring(self):
        return [self.dev(1, 0), self.dev(-1, 0), self.dev(0, 1), self.dev(0, -1)]


class Cuts:
    def __init__(self, c):
        self.c = c
        self.a = (c * 9 // 14) // 8 * 8
        self.b = c - self.a
        self.a0 = (self.a // 2 + 7) // 8 * 8
        self.b0 = (self.b // 2 + 7) // 8 * 8
        self.A = (pl.ds(0, self.a), pl.ds(0, self.a0), pl.ds(self.a0, self.a - self.a0))
        self.B = (
            pl.ds(self.a, self.b),
            pl.ds(self.a, self.b0),
            pl.ds(self.a + self.b0, self.b - self.b0),
        )


AG_SEMS = 6


def ag_sems(nz):
    h = nz // 2
    return [
        pltpu.SemaphoreType.DMA((2, h + 1)),
        pltpu.SemaphoreType.DMA((2, h + 1)),
        pltpu.SemaphoreType.DMA((2, h + 1)),
        pltpu.SemaphoreType.DMA((2, h + 1)),
        pltpu.SemaphoreType.DMA((2, 2, h + 1)),
        pltpu.SemaphoreType.DMA((2, 2, h + 1)),
        pltpu.SemaphoreType.DMA((2, 2, h + 1)),
        pltpu.SemaphoreType.DMA((2, 2, h + 1)),
        pltpu.SemaphoreType.DMA((2, 2)),
        pltpu.SemaphoreType.DMA((2, 2)),
    ]


class Gather:
    def __init__(self, place, out, sems):
        self.p, self.out = place, out
        self.cut = Cuts(out.shape[2])
        self.h = place.nz // 2
        (self.za_s, self.za_r, self.zb_s, self.zb_r, self.xa_s, self.xa_r, self.xh_s, self.xh_r,
         self.xb_s, self.xb_r) = sems

    def za(self, d, s):
        sign = 1 - 2 * d
        src = self.p.zat(-sign * (s - 1))
        rows = self.cut.A[0]
        ref = self.out.at[src, self.p.x, rows, :]
        return copy_to(ref, ref, self.za_s.at[d, s], self.za_r.at[d, s], self.p.dev(sign, 0))

    def za_half(self, d):
        sign = 1 - 2 * d
        src = self.p.zat(-sign * (self.h - 1))
        ref = self.out.at[src, self.p.x, self.cut.A[1 + d], :]
        return copy_to(ref, ref, self.za_s.at[d, self.h], self.za_r.at[d, self.h], self.p.dev(sign, 0))

    def zb(self, d, s):
        sign = 1 - 2 * d
        src = self.p.zat(-sign * (s - 1))
        ref = self.out.at[src, :, self.cut.B[0], :]
        return copy_to(ref, ref, self.zb_s.at[d, s], self.zb_r.at[d, s], self.p.dev(sign, 0))

    def zb_half(self, d):
        sign = 1 - 2 * d
        src = self.p.zat(-sign * (self.h - 1))
        ref = self.out.at[src, pl.ds(d * (NX // 2), NX // 2), self.cut.B[0], :]
        return copy_to(ref, ref, self.zb_s.at[d, self.h], self.zb_r.at[d, self.h], self.p.dev(sign, 0))

    def xa(self, d, g, s):
        src = self.p.zat((2 * g - 1) * s)
        ref = self.out.at[src, self.p.x, self.cut.A[0], :]
        return copy_to(ref, ref, self.xa_s.at[d, g, s], self.xa_r.at[d, g, s], self.p.dev(0, 1 - 2 * d))

    def xh(self, d, g, s):
        sign = 1 - 2 * d
        src = self.p.zat((2 * g - 1) * s)
        ref = self.out.at[src, self.p.xat(-sign), self.cut.A[1 + d], :]
        return copy_to(ref, ref, self.xh_s.at[d, g, s], self.xh_r.at[d, g, s], self.p.dev(0, sign))

    def xb(self, d):
        ref = self.out.at[self.p.z, self.p.x, self.cut.B[0], :]
        return copy_to(ref, ref, self.xb_s.at[0, d], self.xb_r.at[0, d], self.p.dev(0, 1 - 2 * d))

    def xbh(self, d):
        sign = 1 - 2 * d
        ref = self.out.at[self.p.z, self.p.xat(-sign), self.cut.B[1 + d], :]
        return copy_to(ref, ref, self.xb_s.at[1, d], self.xb_r.at[1, d], self.p.dev(0, sign))

    def begin(self):
        for d in (0, 1):
            self.xb(d).start()
            self.za(d, 1).start()
        for d in (0, 1):
            self.xa(d, 0, 0).start()
        for d in (0, 1):
            self.xb(d).wait_recv()
            self.xbh(d).start()
        for d in (0, 1):
            self.xbh(d).wait_recv()
        for d in (0, 1):
            self.zb(d, 1).start()

    def onward(self, g, s):
        for d in (0, 1):
            self.xa(d, g, s).wait_recv()
            self.xh(d, g, s).start()

    def step(self, s):
        for g in (0, 1):
            self.za(g, s).wait_recv()
            self.za(g, s + 1).start()
        for g in (0, 1):
            for d in (0, 1):
                self.xa(d, g, s).start()
        for g in (0, 1):
            self.zb(g, s).wait_recv()
            self.zb(g, s + 1).start()

    def finish(self):
        h = self.h
        s = h - 1
        for g in (0, 1):
            self.za(g, s).wait_recv()
            self.za_half(g).start()
        for g in (0, 1):
            for d in (0, 1):
                self.xa(d, g, s).start()
        for g in (0, 1):
            self.zb(g, s).wait_recv()
            self.zb_half(g).start()
        self.onward(0, s - 1)
        self.onward(1, s - 1)
        for g in (0, 1):
            self.za_half(g).wait_recv()
        for d in (0, 1):
            self.xa(d, 0, h).start()
        self.onward(0, s)
        self.onward(1, s)
        self.onward(0, h)
        for g in (0, 1):
            self.zb_half(g).wait_recv()
        for d in (0, 1):
            self.xh(d, 0, 0).wait()
            self.xh(d, 0, h).wait()
            self.xa(d, 0, 0).wait_send()
            self.xa(d, 0, h).wait_send()
            self.xb(d).wait_send()
            self.xbh(d).wait_send()
            self.za_half(d).wait_send()
            self.zb_half(d).wait_send()

        def drain(i, _):
            for d in (0, 1):
                self.za(d, i).wait_send()
                self.zb(d, i).wait_send()
                for g in (0, 1):
                    self.xa(d, g, i).wait_send()
                    self.xh(d, g, i).wait()
            return _

        lax.fori_loop(1, h, drain, 0)

    def run(self):
        self.begin()
        self.step(1)
        self.onward(0, 0)

        def body(s, _):
            self.step(s)
            self.onward(0, s - 1)
            self.onward(1, s - 1)
            return _

        lax.fori_loop(2, self.h - 1, body, 0)
        self.finish()


def ag_kernel(nz, own_ref, out_ref, *sems):
    place = Place(nz)
    out_ref[place.z, place.x] = own_ref[...]
    greet(place.ring())
    Gather(place, out_ref, sems).run()


def all_gather(own, nz, cid):
    c = own.shape[0]
    return pl.pallas_call(
        functools.partial(ag_kernel, nz),
        out_shape=jax.ShapeDtypeStruct((nz, NX, c, LANE), F32),
        in_specs=[VMEM],
        out_specs=VMEM,
        scratch_shapes=ag_sems(nz),
        compiler_params=pltpu.CompilerParams(
            collective_id=cid, has_side_effects=True, vmem_limit_bytes=48 << 20
        ),
    )(own)


def rs_scratch(nz, c):
    cut = Cuts(c)
    h = nz // 2
    dma = pltpu.SemaphoreType.DMA
    return [
        pltpu.VMEM((2, h + 1, cut.a, LANE), F32),
        pltpu.VMEM((2, h + 1, NX, cut.b, LANE), F32),
        pltpu.VMEM((2, 2, h + 1, cut.a0, LANE), F32),
        pltpu.VMEM((2, 2, h + 1, cut.a, LANE), F32),
        pltpu.VMEM((2, cut.b0, LANE), F32),
        pltpu.VMEM((2, cut.b, LANE), F32),
        dma((2, h + 1)), dma((2, h + 1)), dma((2, h + 1)), dma((2, h + 1)),
        dma((2, 2, h + 1)), dma((2, 2, h + 1)), dma((2, 2, h + 1)), dma((2, 2, h + 1)),
        dma((2, 2)), dma((2, 2)),
    ]


class Scatter:
    def __init__(self, place, part, scratch):
        self.p, self.part = place, part
        self.cut = Cuts(part.shape[2])
        self.h = place.nz // 2
        (self.lza, self.lzb, self.lxh, self.lxa, self.lxbh, self.lxb,
         self.za_s, self.za_r, self.zb_s, self.zb_r,
         self.xh_s, self.xh_r, self.xa_s, self.xa_r, self.xb_s, self.xb_r) = scratch

    def half_len(self, d):
        return self.cut.a0 if d == 0 else self.cut.a - self.cut.a0

    def bhalf_len(self, d):
        return self.cut.b0 if d == 0 else self.cut.b - self.cut.b0

    def xh(self, d, g, s):
        sign = 1 - 2 * d
        zz = self.p.zat((1 - 2 * g) * s)
        return copy_to(
            self.part.at[zz, self.p.xat(2), self.cut.A[1 + d], :],
            self.lxh.at[d, g, s, pl.ds(0, self.half_len(d)), :],
            self.xh_s.at[d, g, s], self.xh_r.at[d, g, s], self.p.dev(0, sign),
        )

    def xa(self, d, g, s):
        sign = 1 - 2 * d
        zz = self.p.zat((1 - 2 * g) * s)
        return copy_to(
            self.part.at[zz, self.p.xat(sign), self.cut.A[0], :],
            self.lxa.at[d, g, s],
            self.xa_s.at[d, g, s], self.xa_r.at[d, g, s], self.p.dev(0, sign),
        )

    def pass_x(self, g, s):
        zz = self.p.zat((1 - 2 * g) * s)
        for d in (0, 1):
            sign = 1 - 2 * d
            self.xh(d, g, s).wait_recv()
            rows = self.cut.A[1 + d]
            xx = self.p.xat(sign)
            self.part[zz, xx, rows, :] = (
                self.part[zz, xx, rows, :] + self.lxh[d, g, s, pl.ds(0, self.half_len(d)), :]
            )
            self.xa(d, g, s).start()

    def sum_x(self, g, s):
        zz = self.p.zat((1 - 2 * g) * s)
        for d in (0, 1):
            self.xa(d, g, s).wait_recv()
        rows = self.cut.A[0]
        self.part[zz, self.p.x, rows, :] = (
            self.part[zz, self.p.x, rows, :] + self.lxa[0, g, s] + self.lxa[1, g, s]
        )

    def za(self, g, s):
        sign = 1 - 2 * g
        return copy_to(
            self.part.at[self.p.zat(sign * s), self.p.x, self.cut.A[0], :],
            self.lza.at[g, s],
            self.za_s.at[g, s], self.za_r.at[g, s], self.p.dev(sign, 0),
        )

    def za_half(self, g):
        sign = 1 - 2 * g
        n = self.half_len(g)
        return copy_to(
            self.part.at[self.p.zat(self.h), self.p.x, self.cut.A[1 + g], :],
            self.lza.at[g, self.h, pl.ds(0, n), :],
            self.za_s.at[g, self.h], self.za_r.at[g, self.h], self.p.dev(sign, 0),
        )

    def zb(self, g, s):
        sign = 1 - 2 * g
        return copy_to(
            self.part.at[self.p.zat(sign * s), :, self.cut.B[0], :],
            self.lzb.at[g, s],
            self.zb_s.at[g, s], self.zb_r.at[g, s], self.p.dev(sign, 0),
        )

    def zb_half(self, g):
        sign = 1 - 2 * g
        xs = pl.ds(g * (NX // 2), NX // 2)
        return copy_to(
            self.part.at[self.p.zat(self.h), xs, self.cut.B[0], :],
            self.lzb.at[g, self.h, pl.ds(0, NX // 2)],
            self.zb_s.at[g, self.h], self.zb_r.at[g, self.h], self.p.dev(sign, 0),
        )

    def xbh(self, d):
        return copy_to(
            self.part.at[self.p.z, self.p.xat(2), self.cut.B[1 + d], :],
            self.lxbh.at[d, pl.ds(0, self.bhalf_len(d)), :],
            self.xb_s.at[0, d], self.xb_r.at[0, d], self.p.dev(0, 1 - 2 * d),
        )

    def xb(self, d):
        sign = 1 - 2 * d
        return copy_to(
            self.part.at[self.p.z, self.p.xat(sign), self.cut.B[0], :],
            self.lxb.at[d],
            self.xb_s.at[1, d], self.xb_r.at[1, d], self.p.dev(0, sign),
        )

    def begin(self):
        h = self.h
        for g in (0, 1):
            self.zb_half(g).start()
        for d in (0, 1):
            self.xh(d, 0, h).start()
        for g in (0, 1):
            for d in (0, 1):
                self.xh(d, g, h - 1).start()
        self.pass_x(0, h)
        for g in (0, 1):
            for d in (0, 1):
                self.xh(d, g, h - 2).start()
        for g in (0, 1):
            self.pass_x(g, h - 1)
        self.sum_x(0, h)
        for g in (0, 1):
            self.za_half(g).start()

    def top(self):
        h = self.h
        s = h - 1
        for g in (0, 1):
            self.zb_half(g).wait_recv()
            zz = self.p.zat((1 - 2 * g) * s)
            xs = pl.ds(g * (NX // 2), NX // 2)
            rows = self.cut.B[0]
            self.part[zz, xs, rows, :] = self.part[zz, xs, rows, :] + self.lzb[g, h, pl.ds(0, NX // 2)]
            self.zb(g, s).start()
        for g in (0, 1):
            for d in (0, 1):
                self.xh(d, g, s - 2).start()
        for g in (0, 1):
            self.pass_x(g, s - 1)
        for g in (0, 1):
            self.sum_x(g, s)
            self.za_half(g).wait_recv()
            zz = self.p.zat((1 - 2 * g) * s)
            rows = self.cut.A[1 + g]
            x = self.p.x
            self.part[zz, x, rows, :] = (
                self.part[zz, x, rows, :] + self.lza[g, h, pl.ds(0, self.half_len(g)), :]
            )
            self.za(g, s).start()

    def ring_b(self, s):
        rows = self.cut.B[0]
        for g in (0, 1):
            self.zb(g, s + 1).wait_recv()
            zz = self.p.zat((1 - 2 * g) * s)
            self.part[zz, :, rows, :] = self.part[zz, :, rows, :] + self.lzb[g, s + 1]
            self.zb(g, s).start()

    def ring_a(self, s):
        rows = self.cut.A[0]
        for g in (0, 1):
            self.sum_x(g, s)
            self.za(g, s + 1).wait_recv()
            zz = self.p.zat((1 - 2 * g) * s)
            self.part[zz, self.p.x, rows, :] = self.part[zz, self.p.x, rows, :] + self.lza[g, s + 1]
            self.za(g, s).start()

    def step(self, s):
        self.ring_b(s)
        if isinstance(s, int) and s <= 2:
            if s == 2:
                for d in (0, 1):
                    self.xh(d, 0, 0).start()
            for g in (0, 1) if s == 2 else (0,):
                self.pass_x(g, s - 1)
        else:
            for g in (0, 1):
                for d in (0, 1):
                    self.xh(d, g, s - 2).start()
            for g in (0, 1):
                self.pass_x(g, s - 1)
        self.ring_a(s)

    def finish(self, out):
        h, cut, p = self.h, self.cut, self.p
        rows = cut.B[0]
        for g in (0, 1):
            self.zb(g, 1).wait_recv()
        self.part[p.z, :, rows, :] = self.part[p.z, :, rows, :] + self.lzb[0, 1] + self.lzb[1, 1]
        for d in (0, 1):
            self.xbh(d).start()
        for d in (0, 1):
            sign = 1 - 2 * d
            self.xbh(d).wait_recv()
            half = cut.B[1 + d]
            xx = p.xat(sign)
            self.part[p.z, xx, half, :] = (
                self.part[p.z, xx, half, :] + self.lxbh[d, pl.ds(0, self.bhalf_len(d)), :]
            )
            self.xb(d).start()
        self.sum_x(0, 0)
        for g in (0, 1):
            self.za(g, 1).wait_recv()
        out[cut.A[0], :] = self.part[p.z, p.x, cut.A[0], :] + self.lza[0, 1] + self.lza[1, 1]
        for d in (0, 1):
            self.xb(d).wait_recv()
        out[rows, :] = self.part[p.z, p.x, rows, :] + self.lxb[0] + self.lxb[1]
        for d in (0, 1):
            self.xh(d, 0, 0).wait_send()
            self.xa(d, 0, 0).wait_send()
            self.xh(d, 0, h).wait_send()
            self.xa(d, 0, h).wait_send()
            self.xb(d).wait_send()
            self.xbh(d).wait_send()
            self.za_half(d).wait_send()
            self.zb_half(d).wait_send()

        def drain(i, _):
            for d in (0, 1):
                self.za(d, i).wait_send()
                self.zb(d, i).wait_send()
                for g in (0, 1):
                    self.xa(d, g, i).wait_send()
                    self.xh(d, g, i).wait_send()
            return _

        lax.fori_loop(1, h, drain, 0)

    def run(self, out):
        self.begin()
        self.top()

        def body(i, _):
            self.step(self.h - 2 - i)
            return _

        lax.fori_loop(0, self.h - 4, body, 0)
        self.step(2)
        self.step(1)
        self.finish(out)


def w_rows(b_ref, l_ref, flat, cols):
    lh, ll = split2(l_ref[...])
    for j in range(0, cols, 256):
        w = dot3(b_ref[:, j : j + 256], (lh, ll), TN)
        for c in range(NX):
            flat[pl.ds(j * NX + c, 256, stride=NX), :] = w[:, c * LANE : (c + 1) * LANE]


def to_chunks(flat, part, c):
    def body(i, _):
        part[i // NX, lax.rem(i, NX)] = flat[pl.ds(pl.multiple_of(i * c, 8), c), :]
        return _

    lax.fori_loop(0, part.shape[0] * NX, body, 0)


def rs_kernel(nz, m_ref, g_ref, l_ref, out_ref, blend, flat, part, *scratch):
    place = Place(nz)
    cols = m_ref.shape[1]
    blend[...] = m_ref[...] + g_ref[...].astype(F32)
    w_rows(blend, l_ref, flat, cols)
    to_chunks(flat, part, out_ref.shape[0])
    greet(place.ring())
    Scatter(place, part, scratch).run(out_ref)


def reduce_scatter(momentum, gradient, left, nz, cid):
    rows, cols = momentum.shape
    c = cols * RANK // LANE // (nz * NX)
    return pl.pallas_call(
        functools.partial(rs_kernel, nz),
        out_shape=jax.ShapeDtypeStruct((c, LANE), F32),
        in_specs=[VMEM] * 3,
        out_specs=VMEM,
        scratch_shapes=[
            pltpu.VMEM((rows, cols), F32),
            pltpu.VMEM((cols * RANK // LANE, LANE), F32),
            pltpu.VMEM((nz, NX, c, LANE), F32),
        ] + rs_scratch(nz, c),
        compiler_params=pltpu.CompilerParams(
            collective_id=cid, has_side_effects=True, vmem_limit_bytes=48 << 20
        ),
    )(momentum, gradient, left)


def left_kernel(nt, m_ref, g_ref, q_ref, out_ref, part, land, s1, r1, s2, r2):
    t = lax.axis_index("tp")
    rows, cols = m_ref.shape
    n = rows // nt
    acc = None
    for j in range(0, cols, 256):
        b = split2(m_ref[:, j : j + 256] + g_ref[:, j : j + 256].astype(F32))
        q = jnp.concatenate(
            [q_ref[pl.ds(j * NX + c, 256, stride=NX), :] for c in range(RANK // LANE)], axis=1
        )
        d = dot3(b, q, NN)
        acc = d if acc is None else acc + d
    part[...] = acc

    def peer(o):
        return lax.rem(t + o, nt)

    greet([{"tp": peer(o)} for o in range(1, nt)])

    def piece(i):
        return pl.ds(pl.multiple_of(i * n, n), n)

    def out1(o):
        return copy_to(part.at[piece(peer(o)), :], land.at[o], s1.at[o], r1.at[o], {"tp": peer(o)})

    def out2(o):
        ref = out_ref.at[piece(t), :]
        return copy_to(ref, ref, s2.at[o], r2.at[o], {"tp": peer(o)})

    for o in range(1, nt):
        out1(o).start()
    total = part[piece(t), :]
    for o in range(1, nt):
        out1(o).wait_recv()
        total = total + land[o]
    out_ref[piece(t), :] = total
    for o in range(1, nt):
        out2(o).start()
    for o in range(1, nt):
        out2(o).wait()
        out1(o).wait_send()


def left_sum(momentum, gradient, q, nt, cid):
    rows = momentum.shape[0]
    dma = pltpu.SemaphoreType.DMA
    return pl.pallas_call(
        functools.partial(left_kernel, nt),
        out_shape=jax.ShapeDtypeStruct((rows, RANK), F32),
        in_specs=[VMEM] * 3,
        out_specs=VMEM,
        scratch_shapes=[
            pltpu.VMEM((rows, RANK), F32),
            pltpu.VMEM((nt, rows // nt, RANK), F32),
            dma((nt,)), dma((nt,)), dma((nt,)), dma((nt,)),
        ],
        compiler_params=pltpu.CompilerParams(
            collective_id=cid, has_side_effects=True, vmem_limit_bytes=48 << 20
        ),
    )(momentum, gradient, q)


def gram_scratch(nz, nt):
    n = RANK // nt // NX
    dma = pltpu.SemaphoreType.DMA
    np_ = n * NX // 8
    return [
        pltpu.VMEM((RANK // nt, RANK), F32),
        pltpu.VMEM((NX, n, RANK), F32),
        pltpu.VMEM((n * NX, LANE), F32),
        pltpu.VMEM((nz, 8, LANE), F32),
        dma((NX,)), dma((NX,)),
        dma((nz,)), dma((nz,)),
        dma((np_,)), dma((np_,)),
        dma((NX,)), dma((NX,)),
        dma((nt,)), dma((nt,)),
    ]


def gram_kernel(nz, nt, l_ref, out_ref, part, landx, flat, landz,
                s1, r1, s2, r2, s3, r3, s4, r4, s5, r5):
    p = Place(nz)
    t = lax.axis_index("tp")
    n = RANK // nt // NX
    pieces = n * NX // 8
    lo = -(pieces // 2)
    offs = [o for o in range(lo, lo + pieces) if o != 0]
    wide = RANK // nt
    left = l_ref[...]
    at = pl.multiple_of(lax.rem(t, LANE // wide) * wide, wide) if wide < LANE else 0
    col = pl.multiple_of(t * wide // LANE * LANE, LANE)
    del at
    tile = l_ref[:, pl.ds(col, LANE)]
    full = dot3(tile, left, TN)
    half = lax.rem(t, LANE // wide)
    mine = full[0:wide]
    for i in range(1, LANE // wide):
        mine = jnp.where(half == i, full[i * wide : (i + 1) * wide], mine)
    part[...] = mine

    greet(
        [p.dev(0, d) for d in range(1, NX)]
        + [p.dev(d, 0) for d in range(1, nz)]
        + [{"tp": lax.rem(t + o, nt)} for o in range(1, nt)]
    )

    def c1(d):
        xx = p.xat(d)
        return copy_to(part.at[pl.ds(pl.multiple_of(xx * n, n), n), :], landx.at[d],
                       s1.at[d], r1.at[d], p.dev(0, d))

    for d in range(1, NX):
        c1(d).start()
    total = part[pl.ds(pl.multiple_of(p.x * n, n), n), :]
    for d in range(1, NX):
        c1(d).wait_recv()
        total = total + landx[d]
    for c in range(RANK // LANE):
        flat[pl.ds(c, n, stride=RANK // LANE), :] = total[:, c * LANE : (c + 1) * LANE]

    def c2(d):
        piece = lax.rem(p.zat(d), pieces)
        return copy_to(flat.at[pl.ds(pl.multiple_of(piece * 8, 8), 8), :], landz.at[p.z],
                       s2.at[d], r2.at[d], p.dev(d, 0))

    for d in range(1, nz):
        c2(d).start()
    own = lax.rem(p.z, pieces)
    landz[p.z] = flat[pl.ds(pl.multiple_of(own * 8, 8), 8), :]
    for d in range(1, nz):
        c2(d).wait_recv()
    tot = landz[0]
    for i in range(1, nz):
        tot = tot + landz[i]
    me = out_ref.at[t, p.x]
    rows = pl.ds(pl.multiple_of(own * 8, 8), 8)
    out_ref[t, p.x, rows, :] = tot

    def c3(i):
        ref = me.at[rows, :]
        return copy_to(ref, ref, s3.at[i], r3.at[i], p.dev(offs[i], 0))

    for i in range(len(offs)):
        c3(i).start()
    for i in range(len(offs)):
        c3(i).wait_recv()

    def c4(d):
        return copy_to(me, me, s4.at[d], r4.at[d], p.dev(0, d))

    for d in range(1, NX):
        c4(d).start()
    for d in range(1, NX):
        c4(d).wait_recv()

    def c5(o):
        ref = out_ref.at[t]
        return copy_to(ref, ref, s5.at[o], r5.at[o], {"tp": lax.rem(t + o, nt)})

    for o in range(1, nt):
        c5(o).start()
    for o in range(1, nt):
        c5(o).wait()
    for d in range(1, NX):
        c4(d).wait_send()
        c1(d).wait_send()
    for i in range(len(offs)):
        c3(i).wait_send()
    for d in range(1, nz):
        c2(d).wait_send()


def gram_sum(left, nz, nt, cid):
    n = RANK // nt // NX
    return pl.pallas_call(
        functools.partial(gram_kernel, nz, nt),
        out_shape=jax.ShapeDtypeStruct((nt, NX, n * RANK // LANE, LANE), F32),
        in_specs=[VMEM],
        out_specs=VMEM,
        scratch_shapes=gram_scratch(nz, nt),
        compiler_params=pltpu.CompilerParams(
            collective_id=cid, has_side_effects=True, vmem_limit_bytes=48 << 20
        ),
    )(left)


BLOCK = 16


def split3(v):
    h = v.astype(BF16)
    r = v - h.astype(F32)
    m = r.astype(BF16)
    return h, m, (r - m.astype(F32)).astype(BF16)


def eliminate(a, at):
    n = a.shape[0]
    wide = a.shape[1] // LANE
    tiles = [a[:, i * LANE : (i + 1) * LANE] for i in range(wide)]
    d = [jnp.broadcast_to(a[:, at + k : at + k + 1], (n, LANE)) for k in range(n)]
    row = lax.broadcasted_iota(jnp.int32, (n, LANE), 0)
    scale = jnp.zeros((n, LANE), F32)
    for k in range(n):
        pivot = d[k][k : k + 1, :]
        r = lax.rsqrt(pivot)
        r = r * (1.5 - 0.5 * pivot * r * r)
        scale = jnp.where(row == k, r, scale)
        if k + 1 < n:
            f = jnp.where(row > k, d[k] * (r * r), 0.0)
            for m in range(k + 1, n):
                d[m] = d[m] - f * d[m][k : k + 1, :]
            tiles = [v - f * v[k : k + 1, :] for v in tiles]
    return jnp.concatenate([v * scale for v in tiles], axis=1)


def chol_panel(zz, p):
    wide = RANK + LANE
    c0 = pl.multiple_of(p * LANE, LANE)
    win = zz.at[pl.ds(c0, LANE), pl.ds(c0, wide)]
    for s in range(0, LANE, BLOCK):
        u = eliminate(win[s : s + BLOCK, :], s)
        win[s : s + BLOCK, :] = u
        if s + BLOCK < LANE:
            h, m, l = split3(u)
            lhs = jnp.concatenate([v[:, :LANE] for v in (h, h, m, h, l, m)], axis=0)
            rhs = jnp.concatenate([h, m, h, l, h, m], axis=0)
            upd = lax.dot_general(lhs, rhs, TN, preferred_element_type=F32)
            win[s + BLOCK :, :] = win[s + BLOCK :, :] - upd[s + BLOCK :, :]

    def below(i, _):
        at = pl.ds(pl.multiple_of(i * LANE, LANE), LANE)
        lhs = zz[pl.ds(c0, LANE), at]
        rest = pl.ds(pl.multiple_of(c0 + LANE, LANE), RANK)
        upd = lax.dot_general(lhs, zz[pl.ds(c0, LANE), rest], TN,
                              precision=lax.Precision.HIGHEST, preferred_element_type=F32)
        zz[at, rest] = zz[at, rest] - upd
        return _

    lax.fori_loop(p + 1, RANK // LANE, below, 0)


def chol_init(zz, g_ref):
    for c in range(RANK // LANE):
        zz[:, c * LANE : (c + 1) * LANE] = g_ref[pl.ds(c, RANK, stride=RANK // LANE), :]
    i = lax.broadcasted_iota(jnp.int32, (RANK, RANK), 0)
    j = lax.broadcasted_iota(jnp.int32, (RANK, RANK), 1)
    zz[:, RANK:] = jnp.where(i == j, 1.0, 0.0).astype(F32)


def chol_kernel(g_ref, out_ref, zz):
    chol_init(zz, g_ref)

    def body(p, _):
        chol_panel(zz, p)
        return _

    lax.fori_loop(0, RANK // LANE, body, 0)
    out_ref[...] = zz[:, RANK:]


def inverse_factor(gram):
    return pl.pallas_call(
        chol_kernel,
        out_shape=jax.ShapeDtypeStruct((RANK, RANK), F32),
        in_specs=[VMEM],
        out_specs=VMEM,
        scratch_shapes=[pltpu.VMEM((RANK, 2 * RANK), F32)],
        compiler_params=pltpu.CompilerParams(vmem_limit_bytes=48 << 20),
    )(gram)


def last_kernel(nt, factor, m_ref, g_ref, l_ref, x_ref, own_ref, w_ref,
                nm_ref, nb_ref, up_ref, wh, wl, sq, land, ss, rs):
    t = lax.axis_index("tp")
    rows, cols = m_ref.shape
    x = split2(x_ref[...])
    total = jnp.zeros((8, RANK), F32)
    for j in range(0, cols, 256):
        w = jnp.concatenate(
            [w_ref[pl.ds(j * NX + c, 256, stride=NX), :] for c in range(RANK // LANE)], axis=1
        )
        h, l = split2(w)
        wh[j : j + 256, :] = h
        wl[j : j + 256, :] = l
        r = dot3((h, l), x, NT)
        total = total + jnp.sum((r * r).reshape(32, 8, RANK), axis=0)
    sq[...] = total

    def peer(o):
        return {"tp": lax.rem(t + o, nt)}

    greet([peer(o) for o in range(1, nt)])

    def send(o):
        return copy_to(sq, land.at[o], ss.at[o], rs.at[o], peer(o))

    for o in range(1, nt):
        send(o).start()
    ortho = dot3(l_ref[...], x, NT)
    m1 = dot3(ortho, x, NN)
    n_own = own_ref.shape[0] // NX
    own = jnp.concatenate(
        [own_ref[pl.ds(c, n_own, stride=NX), :] for c in range(RANK // LANE)], axis=1
    )
    right = dot3(own, x, NT)
    for o in range(1, nt):
        send(o).wait()
        total = total + land[o]
    inv = 1.0 / (jnp.sqrt(jnp.sum(total, axis=0, keepdims=True)) + 1e-06)
    nb_ref[...] = right * inv
    m2 = split2(dot3(ortho * (inv * factor), x, NN))
    m1 = split2(m1 * 0.1)
    for j in range(0, cols, 256):
        w = (wh[j : j + 256, :], wl[j : j + 256, :])
        nm_ref[:, j : j + 256] = (
            m_ref[:, j : j + 256] + g_ref[:, j : j + 256].astype(F32) - dot3(m1, w, NT)
        )
        up_ref[:, j : j + 256] = dot3(m2, w, NT).astype(BF16)


def outputs(momentum, gradient, left, x, own, w, nt, factor, cid):
    rows, cols = momentum.shape
    dma = pltpu.SemaphoreType.DMA
    return pl.pallas_call(
        functools.partial(last_kernel, nt, factor),
        out_shape=(
            jax.ShapeDtypeStruct((rows, cols), F32),
            jax.ShapeDtypeStruct((own.shape[0] // NX, RANK), F32),
            jax.ShapeDtypeStruct((rows, cols), BF16),
        ),
        in_specs=[VMEM] * 6,
        out_specs=(VMEM,) * 3,
        scratch_shapes=[
            pltpu.VMEM((cols, RANK), BF16),
            pltpu.VMEM((cols, RANK), BF16),
            pltpu.VMEM((8, RANK), F32),
            pltpu.VMEM((nt, 8, RANK), F32),
            dma((nt,)), dma((nt,)),
        ],
        compiler_params=pltpu.CompilerParams(
            collective_id=cid, has_side_effects=True, vmem_limit_bytes=48 << 20
        ),
    )(momentum, gradient, left, x, own, w)


def shards(nz, nt, factor, momentum, gradient, right_basis):
    cols = momentum.shape[1]
    q = all_gather(right_basis.reshape(-1, LANE), nz, 1)
    left = left_sum(momentum, gradient, q.reshape(-1, LANE), nt, 2)
    gram = gram_sum(left, nz, nt, 3)
    own = reduce_scatter(momentum, gradient, left, nz, 4)
    w = all_gather(own, nz, 5)
    x = inverse_factor(gram.reshape(-1, LANE))
    return outputs(momentum, gradient, left, x, own, w.reshape(-1, LANE), nt, factor, 6)


def solution(mesh):
    nz = mesh.shape["fsdp"] // NX
    nt = mesh.shape["tp"]
    factor = (float(ROWS) * COLS / RANK) ** 0.5
    placed = (P("fsdp", "tp"), P("fsdp", "tp"), P(("tp", "fsdp"), None))
    return jax.shard_map(
        functools.partial(shards, nz, nt, factor),
        mesh=mesh,
        in_specs=placed,
        out_specs=(P("fsdp", "tp"), P(("tp", "fsdp"), None), P("fsdp", "tp")),
        check_vma=False,
    )
```

time: 1150 us -> 244 us (0.21); the launches traced: 1140 us -> 244 us
  waiting for transfers between devices: 619 us -> 0 us
  blocking collectives: 284 us -> 0 us
  Pallas kernels: 0 us -> 238 us
  other arithmetic: 126 us -> 0 us
  matrix products: 34.9 us -> 0 us
  starting transfers between devices: 28.1 us -> 0 us
  local copies, waits for them, and re-layouts: 26 us -> 5.06 us
  between operations: 17.5 us -> 0.73 us
    psum x2 -> x0, waiting for transfers between devices: 341 us -> none  [the longest x1 264 us: shards(): gram = lax.psum(gram_local, 'fsdp')]
    all_gather x2 -> x0, waiting for transfers between devices: 277 us -> none  [the longest x1 147 us: shards(): lax.all_gather(right_basis, 'fsdp', axis=0, tiled=True)]
    pallas_call x0 -> x7, Pallas kernels: none -> 238 us  [the longest x2 87.7 us: all_gather(): pl.pallas_call(functools.partial(ag_kernel, nz), out_shape=jax.ShapeDtype...]
    psum x1 -> x0, blocking collectives: 143 us -> none  [shards(): squares = lax.psum(jnp.sum(right_part * right_part, axis=0), ('fsdp', 'tp'))]
    unnamed x1 -> x0, blocking collectives: 141 us -> none
    another operation x17 -> x0, other arithmetic: 124 us -> none  [the longest x14 83.6 us: shards(): lower = jnp.linalg.cholesky(gram)]
    unnamed x8 -> x0, starting transfers between devices: 27.7 us -> none
    dot_general x5 -> x0, matrix products: 24.8 us -> none  [the longest x1 6.97 us: shards(): jnp.dot(ortho, basis_block.T, precision=high, preferred_element_type=jnp....]
  transfers between devices with their start and end apart: 12 -> 0, of which waited for: 4 -> 0; matrix products, arithmetic and copies ran while one was open for 0% -> 0% of each run, Pallas kernels for 0% -> 0%
where the time goes in v1:
time: 244 us
  Pallas kernels  238 us (98%)
  local copies, waits for them, and re-layouts  5.06 us (2%)
    pallas_call x2, Pallas kernels, all_gather(): pl.pallas_call(functools.partial(ag_kernel, nz), out_shape=jax.ShapeDtype...  87.7 us
    pallas_call x1, Pallas kernels, gram_sum(): pl.pallas_call(functools.partial(gram_kernel, nz, nt), out_shape=jax.Shap...  44.5 us
    pallas_call x1, Pallas kernels, reduce_scatter(): pl.pallas_call(functools.partial(rs_kernel, nz), out_shape=jax.ShapeDtype...  40.7 us
    pallas_call x1, Pallas kernels, left_sum(): pl.pallas_call(functools.partial(left_kernel, nt), out_shape=jax.ShapeDty...  23.1 us
    pallas_call x1, Pallas kernels, outputs(): pl.pallas_call(functools.partial(last_kernel, nt, factor), out_shape=(jax...  21.6 us
    pallas_call x1, Pallas kernels, inverse_factor(): pl.pallas_call(chol_kernel, out_shape=jax.ShapeDtypeStruct((RANK, RANK),...  20.1 us

profile of v1, /device:TPU:1, one launch (start us, length us, event | category | flops | bytes accessed | tf_op | source)
XLA Modules:
  0.0 243.6 jit_solution(3398468388078010943)
XLA Ops:
  0.6 0.0 copy-start.2
  0.6 0.0 copy-start.1
  0.7 0.9 reshape.18.own_ref
  1.6 49.1 %shard_map.58 = f32[16,4,112,128]{3,2,1,0:T(8,128)S(1)} custom-call(f32[112,128]{1,0:T(8,128)S(1)} %reshape.18.own_ref), custom_call_target="tpu_custom_call" | custom-call | tf_op jit(solution)/shard_map/pallas_call | solution.py:254
  50.8 0.0 copy-done.2
  50.8 0.0 copy-done.1
  50.8 23.1 %shard_map.59.l_ref = f32[128,512]{1,0:T(8,128)S(1)} custom-call(f32[128,1792]{1,0:T(8,128)S(1)} %copy-done.1, bf16[128,1792]{1,0:T(8,128)(2,1)S(1)} %copy-done.2, f32[7168,128]{1,0:T(8,128)S(1)} %bitcast.4), custom_call_target="tpu_custom_call" | custom-call | tf_op jit(solution)/shard_map/pallas_call | solution.py:614
  73.9 40.7 %shard_map.62.own_ref = f32[112,128]{1,0:T(8,128)S(1)} custom-call(f32[128,1792]{1,0:T(8,128)S(1)} %copy-done.1, bf16[128,1792]{1,0:T(8,128)(2,1)S(1)} %copy-done.2, f32[128,512]{1,0:T(8,128)S(1)} %shard_map.59.l_ref), custom_call_target="tpu_custom_call" | custom-call | tf_op jit(solution)/shard_map/pallas_call | solution.py:552
  114.7 44.5 %shard_map.60 = f32[8,4,64,128]{3,2,1,0:T(8,128)S(1)} custom-call(f32[128,512]{1,0:T(8,128)S(1)} %shard_map.59.l_ref), custom_call_target="tpu_custom_call" | custom-call | tf_op jit(solution)/shard_map/pallas_call | solution.py:742
  159.2 20.1 %shard_map.61.x_ref = f32[512,512]{1,0:T(8,128)S(1)} custom-call(f32[2048,128]{1,0:T(8,128)S(1)} %bitcast.5), custom_call_target="tpu_custom_call" | custom-call | tf_op jit(solution)/shard_map/pallas_call | solution.py:830
  179.3 38.6 %shard_map.63 = f32[16,4,112,128]{3,2,1,0:T(8,128)S(1)} custom-call(f32[112,128]{1,0:T(8,128)S(1)} %shard_map.62.own_ref), custom_call_target="tpu_custom_call" | custom-call | tf_op jit(solution)/shard_map/pallas_call | solution.py:254
  217.8 0.0 copy-start
  217.8 1.8 copy-done
  219.6 21.6 %shard_map.64 = (f32[128,1792]{1,0:T(8,128)S(1)}, f32[28,512]{1,0:T(8,128)S(1)}, bf16[128,1792]{1,0:T(8,128)(2,1)S(1)}) custom-call(f32[128,1792]{1,0:T(8,128)S(1)} %copy-done.1, bf16[128,1792]{1,0:T(8,128)(2,1)S(1)} %copy-done.2, f32[128,512]{1,0:T(8,128)S(1)} %shard_map.59.l_ref, f32[512,512]{1,0:T(8,128)S(1)} %shard_map.61.x_ref, ...), custom_call_target="tpu_custom_call" | custom-call | tf_op jit(solution)/shard_map/pallas_call | solution.py:892
  241.2 0.9 copy.9
  242.2 0.6 copy.10
  242.8 0.8 copy.11
Async XLA Ops:
  0.6 50.1 %copy-start.2 = (bf16[128,1792]{1,0:T(8,128)(2,1)S(1)}, bf16[128,1792]{1,0:T(8,128)(2,1)}, u32[]{:S(2)}) copy-start(bf16[128,1792]{1,0:T(8,128)(2,1)} %g_ref.5) | copy-start | bytes 1376260
  0.6 50.1 %copy-start.1 = (f32[128,1792]{1,0:T(8,128)S(1)}, f32[128,1792]{1,0:T(8,128)}, u32[]{:S(2)}) copy-start(f32[128,1792]{1,0:T(8,128)} %m_ref.5) | copy-start | bytes 2752516
  217.8 1.8 copy-start

commit v2 on v0

v2 whole, which is shorter than its diff:
```python
import functools

import jax
import jax.numpy as jnp
from jax import lax
from jax.experimental import pallas as pl
from jax.experimental.pallas import tpu as pltpu
from jax.sharding import PartitionSpec as P

ROWS = 8192
COLS = 14336
RANK = 512
MESH = pl.DeviceIdType.MESH
LANE = 128
NX = 4
VMEM = pl.BlockSpec(memory_space=pltpu.VMEM)
F32 = jnp.float32
BF16 = jnp.bfloat16
NN = (((1,), (0,)), ((), ()))
TN = (((0,), (0,)), ((), ()))
NT = (((1,), (1,)), ((), ()))


def split2(v):
    hi = v.astype(BF16)
    return hi, (v - hi.astype(F32)).astype(BF16)


def dot3(a, b, dims):
    ah, al = a if isinstance(a, tuple) else split2(a)
    bh, bl = b if isinstance(b, tuple) else split2(b)
    d = functools.partial(lax.dot_general, dimension_numbers=dims, preferred_element_type=F32)
    return d(ah, bh) + (d(ah, bl) + d(al, bh))


def copy_to(src, dst, send, recv, where):
    return pltpu.make_async_remote_copy(
        src_ref=src, dst_ref=dst, send_sem=send, recv_sem=recv, device_id=where, device_id_type=MESH
    )


def greet(peers):
    barrier = pltpu.get_barrier_semaphore()
    for peer in peers:
        pl.semaphore_signal(barrier, inc=1, device_id=peer, device_id_type=MESH)
    pl.semaphore_wait(barrier, len(peers))


class Place:
    def __init__(self, nz):
        me = lax.axis_index("fsdp")
        self.nz = nz
        self.z = me // NX
        self.x = lax.rem(me, NX)

    def zat(self, d):
        return lax.rem(self.z + (d + self.nz), self.nz)

    def xat(self, d):
        return lax.rem(self.x + (d + NX), NX)

    def dev(self, dz, dx):
        return {"fsdp": self.zat(dz) * NX + self.xat(dx)}

    def near(self):
        zs = NEAR + (3, -3, HUB, -HUB)
        return [self.dev(d, 0) for d in zs] + [self.dev(0, 1), self.dev(0, -1)]


HUB = 5
NEAR = (1, -1, 2, -2)
FAR = (4, -4, 6, -6, 3, -3, 7, -7, 8)
NOFF = 17


def halves(c):
    return (pl.ds(0, c // 2), pl.ds(c // 2, c // 2))


def ag_sems():
    dma = pltpu.SemaphoreType.DMA
    return [dma((NOFF,)), dma((NOFF,))] + [dma((2, NOFF))] * 4


class Gather:
    order = NEAR + (HUB, -HUB) + FAR

    def __init__(self, place, out, sems):
        self.p, self.out = place, out
        self.half = halves(out.shape[2])
        self.zs, self.zr, self.xs, self.xr, self.hs, self.hr = sems

    def zc(self, o):
        p, i = self.p, o + 8
        if o in NEAR or abs(o) == HUB:
            ref, to = self.out.at[p.z, p.x], o
        else:
            hub = HUB if o > 0 else -HUB
            ref, to = self.out.at[p.zat(-hub), p.x], o - hub
            if abs(o) == 8:
                ref = ref.at[self.half[0 if o > 0 else 1], :]
        return copy_to(ref, ref, self.zs.at[i], self.zr.at[i], p.dev(to, 0))

    def xa(self, d, o):
        ref = self.out.at[self.p.zat(-o), self.p.x]
        return copy_to(ref, ref, self.xs.at[d, o + 8], self.xr.at[d, o + 8], self.p.dev(0, 1 - 2 * d))

    def xh(self, d, o):
        sign = 1 - 2 * d
        ref = self.out.at[self.p.zat(-o), self.p.xat(-sign), self.half[d], :]
        return copy_to(ref, ref, self.hs.at[d, o + 8], self.hr.at[d, o + 8], self.p.dev(0, sign))

    def begin(self):
        for d in (0, 1):
            self.xa(d, 0).start()
        for o in (HUB, -HUB) + NEAR:
            self.zc(o).start()

    def arrive(self, o):
        self.zc(o).wait_recv()
        if abs(o) == HUB:
            for j in NEAR + ((3,) if o > 0 else (-3,)):
                self.zc(o + j).start()
        if o == 8:
            self.zc(-8).wait_recv()
        for d in (0, 1):
            self.xa(d, o).start()

    def onward(self, o):
        for d in (0, 1):
            self.xa(d, o).wait_recv()
            self.xh(d, o).start()

    def events(self):
        lag = 3
        out = []
        groups = (0,) + self.order
        for i in range(1, len(groups) + lag):
            todo = []
            if i < len(groups):
                todo.append(functools.partial(self.arrive, groups[i]))
            if 0 <= i - lag < len(groups):
                todo.append(functools.partial(self.onward, groups[i - lag]))
            out.append(todo)
        return out

    def finish(self):
        for o in (0,) + self.order:
            for d in (0, 1):
                self.xh(d, o).wait()
                self.xa(d, o).wait_send()
            if o:
                self.zc(o).wait_send()
        self.zc(-8).wait_send()


def ag_kernel(nz, own_ref, out_ref, *sems):
    place = Place(nz)
    out_ref[place.z, place.x] = own_ref[...]
    greet(place.near())
    gather = Gather(place, out_ref, sems)
    gather.begin()
    for todo in gather.events():
        for f in todo:
            f()
    gather.finish()


def all_gather(own, nz, cid):
    c = own.shape[0]
    return pl.pallas_call(
        functools.partial(ag_kernel, nz),
        out_shape=jax.ShapeDtypeStruct((nz, NX, c, LANE), F32),
        in_specs=[VMEM],
        out_specs=VMEM,
        scratch_shapes=ag_sems(),
        compiler_params=pltpu.CompilerParams(
            collective_id=cid, has_side_effects=True, vmem_limit_bytes=48 << 20
        ),
    )(own)


def ag_chol_kernel(nz, own_ref, g_ref, out_ref, x_ref, zz, *sems):
    place = Place(nz)
    out_ref[place.z, place.x] = own_ref[...]
    greet(place.near())
    gather = Gather(place, out_ref, sems)
    gather.begin()
    chol_init(zz, g_ref)
    events = gather.events()
    blocks = LANE // BLOCK

    def between(p, s):
        for pp in range(RANK // LANE):
            at = pp * blocks + s
            if at % 2 == 1 and at // 2 < len(events):

                @pl.when(p == pp)
                def _(at=at):
                    for f in events[at // 2]:
                        f()

    def body(p, _):
        chol_panel(zz, p, between)
        return _

    lax.fori_loop(0, RANK // LANE, body, 0)
    for todo in events[RANK // BLOCK // 2 :]:
        for f in todo:
            f()
    x_ref[...] = zz[:, RANK:]
    gather.finish()


def gather_and_factor(own, gram, nz, cid):
    c = own.shape[0]
    return pl.pallas_call(
        functools.partial(ag_chol_kernel, nz),
        out_shape=(
            jax.ShapeDtypeStruct((nz, NX, c, LANE), F32),
            jax.ShapeDtypeStruct((RANK, RANK), F32),
        ),
        in_specs=[VMEM] * 2,
        out_specs=(VMEM,) * 2,
        scratch_shapes=[pltpu.VMEM((RANK, 2 * RANK), F32)] + ag_sems(),
        compiler_params=pltpu.CompilerParams(
            collective_id=cid, has_side_effects=True, vmem_limit_bytes=48 << 20
        ),
    )(own, gram)


def rs_scratch(c):
    dma = pltpu.SemaphoreType.DMA
    return [
        pltpu.VMEM((NOFF, c, LANE), F32),
        pltpu.VMEM((2, NOFF, c // 2, LANE), F32),
        pltpu.VMEM((2, NOFF, c, LANE), F32),
        dma((NOFF,)), dma((NOFF,)),
    ] + [dma((2, NOFF))] * 4


class Scatter:
    order = (8, 3, -3, 4, -4, 6, -6, 7, -7, HUB, -HUB, 1, -1, 2, -2, 0)

    def __init__(self, place, part, scratch):
        self.p, self.part = place, part
        self.half = halves(part.shape[2])
        self.n = part.shape[2]
        self.lz, self.lh, self.la, self.zs, self.zr, self.xs, self.xr, self.hs, self.hr = scratch

    def xh(self, d, o):
        p = self.p
        return copy_to(
            self.part.at[p.zat(o), p.xat(2), self.half[d], :], self.lh.at[d, o + 8],
            self.hs.at[d, o + 8], self.hr.at[d, o + 8], p.dev(0, 1 - 2 * d),
        )

    def xa(self, d, o):
        p, sign = self.p, 1 - 2 * d
        return copy_to(
            self.part.at[p.zat(o), p.xat(sign)], self.la.at[d, o + 8],
            self.xs.at[d, o + 8], self.xr.at[d, o + 8], p.dev(0, sign),
        )

    def zc(self, o):
        p, i = self.p, o + 8
        ref, land, to = self.part.at[p.zat(o), p.x], self.lz.at[i], o
        if o not in NEAR and abs(o) != HUB:
            to = o - (HUB if o > 0 else -HUB)
            if abs(o) == 8:
                rows = self.half[0 if o > 0 else 1]
                ref, land = ref.at[rows, :], land.at[rows, :]
        return copy_to(ref, land, self.zs.at[i], self.zr.at[i], p.dev(to, 0))

    def ahead(self, o):
        for d in (0, 1):
            self.xh(d, o).start()

    def pass_x(self, o):
        p = self.p
        zz = p.zat(o)
        for d in (0, 1):
            self.xh(d, o).wait_recv()
            rows, xx = self.half[d], p.xat(1 - 2 * d)
            self.part[zz, xx, rows, :] = self.part[zz, xx, rows, :] + self.lh[d, o + 8]
            self.xa(d, o).start()

    def sum_x(self, o):
        p = self.p
        zz = p.zat(o)
        for d in (0, 1):
            self.xa(d, o).wait_recv()
        self.part[zz, p.x] = self.part[zz, p.x] + self.la[0, o + 8] + self.la[1, o + 8]
        if o == 8:
            self.zc(8).start()
            self.zc(-8).start()
        elif o and abs(o) != HUB:
            self.zc(o).start()

    def hub(self, o):
        p = self.p
        zz = p.zat(o)
        total = self.part[zz, p.x]
        for j in NEAR:
            self.zc(o + j).wait_recv()
            total = total + self.lz[o + j + 8]
        self.part[zz, p.x] = total
        i = 0 if o > 0 else 1
        end = 8 if o > 0 else -8
        self.zc(end).wait_recv()
        rows = self.half[i]
        self.part[zz, p.x, rows, :] = self.part[zz, p.x, rows, :] + self.lz[end + 8, rows, :]
        self.zc(o).start()

    def run(self, out, others):
        g = self.order
        lag = 3
        for o in g[:lag]:
            self.ahead(o)
        for i in range(len(g) + lag):
            if i + lag < len(g):
                self.ahead(g[i + lag])
            if i < len(g):
                self.pass_x(g[i])
            if i >= lag:
                self.sum_x(g[i - lag])
                if g[i - lag] == 1:
                    self.hub(HUB)
                if g[i - lag] == -1:
                    self.hub(-HUB)
            if i in others:
                others[i]()
        total = self.part[self.p.z, self.p.x]
        for o in NEAR + (HUB, -HUB):
            self.zc(o).wait_recv()
            total = total + self.lz[o + 8]
        out[...] = total
        for o in g:
            for d in (0, 1):
                self.xh(d, o).wait_send()
                self.xa(d, o).wait_send()
            if o:
                self.zc(o).wait_send()
        self.zc(-8).wait_send()


def w_rows(b_ref, l_ref, flat, cols):
    lh, ll = split2(l_ref[...])
    for j in range(0, cols, 256):
        w = dot3(b_ref[:, j : j + 256], (lh, ll), TN)
        for c in range(NX):
            flat[pl.ds(j * NX + c, 256, stride=NX), :] = w[:, c * LANE : (c + 1) * LANE]


def to_chunks(flat, part, c):
    def body(i, _):
        part[i // NX, lax.rem(i, NX)] = flat[pl.ds(pl.multiple_of(i * c, 8), c), :]
        return _

    lax.fori_loop(0, part.shape[0] * NX, body, 0)


def rs_kernel(nz, nt, m_ref, g_ref, l_ref, out_ref, gram_ref, blend, flat, part, *scratch):
    place = Place(nz)
    cols = m_ref.shape[1]
    n_rs = len(rs_scratch(8))
    gram = Gram(place, nt, gram_ref, scratch[n_rs:])
    gram.compute(l_ref)
    zs = [place.dev(d, 0) for d in range(1, nz)]
    xs = [place.dev(0, d) for d in range(1, NX)]
    greet(zs + xs + [gram.peer(o) for o in range(1, nt)])
    gram.stage1()
    blend[...] = m_ref[...] + g_ref[...].astype(F32)
    w_rows(blend, l_ref, flat, cols)
    to_chunks(flat, part, out_ref.shape[0])
    gram.stage2()
    others = {3: gram.stage3, 6: gram.stage4, 9: gram.stage5}
    Scatter(place, part, scratch[:n_rs]).run(out_ref, others)
    gram.finish()


def scatter_and_gram(momentum, gradient, left, nz, nt, cid):
    rows, cols = momentum.shape
    c = cols * RANK // LANE // (nz * NX)
    n = RANK // nt // NX
    return pl.pallas_call(
        functools.partial(rs_kernel, nz, nt),
        out_shape=(
            jax.ShapeDtypeStruct((c, LANE), F32),
            jax.ShapeDtypeStruct((nt, NX, n * RANK // LANE, LANE), F32),
        ),
        in_specs=[VMEM] * 3,
        out_specs=(VMEM,) * 2,
        scratch_shapes=[
            pltpu.VMEM((rows, cols), F32),
            pltpu.VMEM((cols * RANK // LANE, LANE), F32),
            pltpu.VMEM((nz, NX, c, LANE), F32),
        ] + rs_scratch(c) + gram_scratch(nz, nt),
        compiler_params=pltpu.CompilerParams(
            collective_id=cid, has_side_effects=True, vmem_limit_bytes=48 << 20
        ),
    )(momentum, gradient, left)


def left_kernel(nt, m_ref, g_ref, q_ref, out_ref, part, land, s1, r1, s2, r2):
    t = lax.axis_index("tp")
    rows, cols = m_ref.shape
    n = rows // nt
    acc = None
    for j in range(0, cols, 256):
        b = split2(m_ref[:, j : j + 256] + g_ref[:, j : j + 256].astype(F32))
        q = jnp.concatenate(
            [q_ref[pl.ds(j * NX + c, 256, stride=NX), :] for c in range(RANK // LANE)], axis=1
        )
        d = dot3(b, q, NN)
        acc = d if acc is None else acc + d
    part[...] = acc

    def peer(o):
        return lax.rem(t + o, nt)

    greet([{"tp": peer(o)} for o in range(1, nt)])

    def piece(i):
        return pl.ds(pl.multiple_of(i * n, n), n)

    def out1(o):
        return copy_to(part.at[piece(peer(o)), :], land.at[o], s1.at[o], r1.at[o], {"tp": peer(o)})

    def out2(o):
        ref = out_ref.at[piece(t), :]
        return copy_to(ref, ref, s2.at[o], r2.at[o], {"tp": peer(o)})

    for o in range(1, nt):
        out1(o).start()
    total = part[piece(t), :]
    for o in range(1, nt):
        out1(o).wait_recv()
        total = total + land[o]
    out_ref[piece(t), :] = total
    for o in range(1, nt):
        out2(o).start()
    for o in range(1, nt):
        out2(o).wait()
        out1(o).wait_send()


def left_sum(momentum, gradient, q, nt, cid):
    rows = momentum.shape[0]
    dma = pltpu.SemaphoreType.DMA
    return pl.pallas_call(
        functools.partial(left_kernel, nt),
        out_shape=jax.ShapeDtypeStruct((rows, RANK), F32),
        in_specs=[VMEM] * 3,
        out_specs=VMEM,
        scratch_shapes=[
            pltpu.VMEM((rows, RANK), F32),
            pltpu.VMEM((nt, rows // nt, RANK), F32),
            dma((nt,)), dma((nt,)), dma((nt,)), dma((nt,)),
        ],
        compiler_params=pltpu.CompilerParams(
            collective_id=cid, has_side_effects=True, vmem_limit_bytes=48 << 20
        ),
    )(momentum, gradient, q)


def gram_scratch(nz, nt):
    n = RANK // nt // NX
    dma = pltpu.SemaphoreType.DMA
    np_ = n * NX // 8
    return [
        pltpu.VMEM((RANK // nt, RANK), F32),
        pltpu.VMEM((NX, n, RANK), F32),
        pltpu.VMEM((n * NX, LANE), F32),
        pltpu.VMEM((nz, 8, LANE), F32),
        dma((NX,)), dma((NX,)),
        dma((nz,)), dma((nz,)),
        dma((np_,)), dma((np_,)),
        dma((NX,)), dma((NX,)),
        dma((nt,)), dma((nt,)),
    ]


class Gram:
    def __init__(self, place, nt, out, scratch):
        self.p, self.nt, self.out = place, nt, out
        (self.part, self.landx, self.flat, self.landz, self.s1, self.r1, self.s2, self.r2,
         self.s3, self.r3, self.s4, self.r4, self.s5, self.r5) = scratch
        self.t = lax.axis_index("tp")
        self.n = RANK // nt // NX
        self.pieces = self.n * NX // 8
        lo = -(self.pieces // 2)
        self.offs = [o for o in range(lo, lo + self.pieces) if o != 0]
        self.own = lax.rem(place.z, self.pieces)
        self.me = out.at[self.t, place.x]
        self.rows = pl.ds(pl.multiple_of(self.own * 8, 8), 8)

    def peer(self, o):
        return {"tp": lax.rem(self.t + o, self.nt)}

    def compute(self, l_ref):
        wide = RANK // self.nt
        col = pl.multiple_of(self.t * wide // LANE * LANE, LANE)
        full = dot3(l_ref[:, pl.ds(col, LANE)], l_ref[...], TN)
        which = lax.rem(self.t, LANE // wide)
        mine = full[0:wide]
        for i in range(1, LANE // wide):
            mine = jnp.where(which == i, full[i * wide : (i + 1) * wide], mine)
        self.part[...] = mine

    def c1(self, d):
        xx = self.p.xat(d)
        n = self.n
        return copy_to(self.part.at[pl.ds(pl.multiple_of(xx * n, n), n), :], self.landx.at[d],
                       self.s1.at[d], self.r1.at[d], self.p.dev(0, d))

    def c2(self, d):
        piece = lax.rem(self.p.zat(d), self.pieces)
        return copy_to(self.flat.at[pl.ds(pl.multiple_of(piece * 8, 8), 8), :],
                       self.landz.at[self.p.z], self.s2.at[d], self.r2.at[d], self.p.dev(d, 0))

    def c3(self, i):
        ref = self.me.at[self.rows, :]
        return copy_to(ref, ref, self.s3.at[i], self.r3.at[i], self.p.dev(self.offs[i], 0))

    def c4(self, d):
        return copy_to(self.me, self.me, self.s4.at[d], self.r4.at[d], self.p.dev(0, d))

    def c5(self, o):
        ref = self.out.at[self.t]
        return copy_to(ref, ref, self.s5.at[o], self.r5.at[o], self.peer(o))

    def stage1(self):
        for d in range(1, NX):
            self.c1(d).start()

    def stage2(self):
        n = self.n
        total = self.part[pl.ds(pl.multiple_of(self.p.x * n, n), n), :]
        for d in range(1, NX):
            self.c1(d).wait_recv()
            total = total + self.landx[d]
        for c in range(RANK // LANE):
            self.flat[pl.ds(c, n, stride=RANK // LANE), :] = total[:, c * LANE : (c + 1) * LANE]
        for d in range(1, self.p.nz):
            self.c2(d).start()
        self.landz[self.p.z] = self.flat[self.rows, :]

    def stage3(self):
        for d in range(1, self.p.nz):
            self.c2(d).wait_recv()
        tot = self.landz[0]
        for i in range(1, self.p.nz):
            tot = tot + self.landz[i]
        self.out[self.t, self.p.x, self.rows, :] = tot
        for i in range(len(self.offs)):
            self.c3(i).start()

    def stage4(self):
        for i in range(len(self.offs)):
            self.c3(i).wait_recv()
        for d in range(1, NX):
            self.c4(d).start()

    def stage5(self):
        for d in range(1, NX):
            self.c4(d).wait_recv()
        for o in range(1, self.nt):
            self.c5(o).start()

    def finish(self):
        for o in range(1, self.nt):
            self.c5(o).wait()
        for d in range(1, NX):
            self.c4(d).wait_send()
            self.c1(d).wait_send()
        for i in range(len(self.offs)):
            self.c3(i).wait_send()
        for d in range(1, self.p.nz):
            self.c2(d).wait_send()


BLOCK = 16


def split3(v):
    h = v.astype(BF16)
    r = v - h.astype(F32)
    m = r.astype(BF16)
    return h, m, (r - m.astype(F32)).astype(BF16)


def eliminate(a, at):
    n = a.shape[0]
    wide = a.shape[1] // LANE
    tiles = [a[:, i * LANE : (i + 1) * LANE] for i in range(wide)]
    d = [jnp.broadcast_to(a[:, at + k : at + k + 1], (n, LANE)) for k in range(n)]
    row = lax.broadcasted_iota(jnp.int32, (n, LANE), 0)
    scale = jnp.zeros((n, LANE), F32)
    for k in range(n):
        pivot = d[k][k : k + 1, :]
        r = lax.rsqrt(pivot)
        r = r * (1.5 - 0.5 * pivot * r * r)
        scale = jnp.where(row == k, r, scale)
        if k + 1 < n:
            f = jnp.where(row > k, d[k] * (r * r), 0.0)
            for m in range(k + 1, n):
                d[m] = d[m] - f * d[m][k : k + 1, :]
            tiles = [v - f * v[k : k + 1, :] for v in tiles]
    return jnp.concatenate([v * scale for v in tiles], axis=1)


def chol_panel(zz, p, between):
    wide = RANK + LANE
    c0 = pl.multiple_of(p * LANE, LANE)
    win = zz.at[pl.ds(c0, LANE), pl.ds(c0, wide)]
    for s in range(0, LANE, BLOCK):
        u = eliminate(win[s : s + BLOCK, :], s)
        win[s : s + BLOCK, :] = u
        if s + BLOCK < LANE:
            h, m, l = split3(u)
            lhs = jnp.concatenate([v[:, :LANE] for v in (h, h, m, h, l, m)], axis=0)
            rhs = jnp.concatenate([h, m, h, l, h, m], axis=0)
            upd = lax.dot_general(lhs, rhs, TN, preferred_element_type=F32)
            win[s + BLOCK :, :] = win[s + BLOCK :, :] - upd[s + BLOCK :, :]
        between(p, s // BLOCK)

    def below(i, _):
        at = pl.ds(pl.multiple_of(i * LANE, LANE), LANE)
        lhs = zz[pl.ds(c0, LANE), at]
        rest = pl.ds(pl.multiple_of(c0 + LANE, LANE), RANK)
        upd = lax.dot_general(lhs, zz[pl.ds(c0, LANE), rest], TN,
                              precision=lax.Precision.HIGHEST, preferred_element_type=F32)
        zz[at, rest] = zz[at, rest] - upd
        return _

    lax.fori_loop(p + 1, RANK // LANE, below, 0)


def chol_init(zz, g_ref):
    for c in range(RANK // LANE):
        zz[:, c * LANE : (c + 1) * LANE] = g_ref[pl.ds(c, RANK, stride=RANK // LANE), :]
    i = lax.broadcasted_iota(jnp.int32, (RANK, RANK), 0)
    j = lax.broadcasted_iota(jnp.int32, (RANK, RANK), 1)
    zz[:, RANK:] = jnp.where(i == j, 1.0, 0.0).astype(F32)


def last_kernel(nt, factor, m_ref, g_ref, l_ref, x_ref, own_ref, w_ref,
                nm_ref, nb_ref, up_ref, wh, wl, sq, land, ss, rs):
    t = lax.axis_index("tp")
    rows, cols = m_ref.shape
    x = split2(x_ref[...])
    total = jnp.zeros((8, RANK), F32)
    for j in range(0, cols, 256):
        w = jnp.concatenate(
            [w_ref[pl.ds(j * NX + c, 256, stride=NX), :] for c in range(RANK // LANE)], axis=1
        )
        h, l = split2(w)
        wh[j : j + 256, :] = h
        wl[j : j + 256, :] = l
        r = dot3((h, l), x, NT)
        total = total + jnp.sum((r * r).reshape(32, 8, RANK), axis=0)
    sq[...] = total

    def peer(o):
        return {"tp": lax.rem(t + o, nt)}

    greet([peer(o) for o in range(1, nt)])

    def send(o):
        return copy_to(sq, land.at[o], ss.at[o], rs.at[o], peer(o))

    for o in range(1, nt):
        send(o).start()
    ortho = dot3(l_ref[...], x, NT)
    m1 = dot3(ortho, x, NN)
    n_own = own_ref.shape[0] // NX
    own = jnp.concatenate(
        [own_ref[pl.ds(c, n_own, stride=NX), :] for c in range(RANK // LANE)], axis=1
    )
    right = dot3(own, x, NT)
    for o in range(1, nt):
        send(o).wait()
        total = total + land[o]
    inv = 1.0 / (jnp.sqrt(jnp.sum(total, axis=0, keepdims=True)) + 1e-06)
    nb_ref[...] = right * inv
    m2 = split2(dot3(ortho * (inv * factor), x, NN))
    m1 = split2(m1 * 0.1)
    for j in range(0, cols, 256):
        w = (wh[j : j + 256, :], wl[j : j + 256, :])
        nm_ref[:, j : j + 256] = (
            m_ref[:, j : j + 256] + g_ref[:, j : j + 256].astype(F32) - dot3(m1, w, NT)
        )
        up_ref[:, j : j + 256] = dot3(m2, w, NT).astype(BF16)


def outputs(momentum, gradient, left, x, own, w, nt, factor, cid):
    rows, cols = momentum.shape
    dma = pltpu.SemaphoreType.DMA
    return pl.pallas_call(
        functools.partial(last_kernel, nt, factor),
        out_shape=(
            jax.ShapeDtypeStruct((rows, cols), F32),
            jax.ShapeDtypeStruct((own.shape[0] // NX, RANK), F32),
            jax.ShapeDtypeStruct((rows, cols), BF16),
        ),
        in_specs=[VMEM] * 6,
        out_specs=(VMEM,) * 3,
        scratch_shapes=[
            pltpu.VMEM((cols, RANK), BF16),
            pltpu.VMEM((cols, RANK), BF16),
            pltpu.VMEM((8, RANK), F32),
            pltpu.VMEM((nt, 8, RANK), F32),
            dma((nt,)), dma((nt,)),
        ],
        compiler_params=pltpu.CompilerParams(
            collective_id=cid, has_side_effects=True, vmem_limit_bytes=48 << 20
        ),
    )(momentum, gradient, left, x, own, w)


def shards(nz, nt, factor, momentum, gradient, right_basis):
    cols = momentum.shape[1]
    q = all_gather(right_basis.reshape(-1, LANE), nz, 1)
    left = left_sum(momentum, gradient, q.reshape(-1, LANE), nt, 2)
    own, gram = scatter_and_gram(momentum, gradient, left, nz, nt, 3)
    w, x = gather_and_factor(own, gram.reshape(-1, LANE), nz, 4)
    return outputs(momentum, gradient, left, x, own, w.reshape(-1, LANE), nt, factor, 5)


def solution(mesh):
    nz = mesh.shape["fsdp"] // NX
    nt = mesh.shape["tp"]
    factor = (float(ROWS) * COLS / RANK) ** 0.5
    placed = (P("fsdp", "tp"), P("fsdp", "tp"), P(("tp", "fsdp"), None))
    return jax.shard_map(
        functools.partial(shards, nz, nt, factor),
        mesh=mesh,
        in_specs=placed,
        out_specs=(P("fsdp", "tp"), P(("tp", "fsdp"), None), P("fsdp", "tp")),
        check_vma=False,
    )
```

time: 1150 us -> 192 us (0.17); the launches traced: 1140 us -> 192 us
  waiting for transfers between devices: 619 us -> 0 us
  blocking collectives: 284 us -> 0 us
  Pallas kernels: 0 us -> 186 us
  other arithmetic: 126 us -> 0 us
  matrix products: 34.9 us -> 0 us
  starting transfers between devices: 28.1 us -> 0 us
  local copies, waits for them, and re-layouts: 26 us -> 5.07 us
  between operations: 17.5 us -> 0.71 us
    psum x2 -> x0, waiting for transfers between devices: 341 us -> none  [the longest x1 264 us: shards(): gram = lax.psum(gram_local, 'fsdp')]
    all_gather x2 -> x0, waiting for transfers between devices: 277 us -> none  [the longest x1 147 us: shards(): lax.all_gather(right_basis, 'fsdp', axis=0, tiled=True)]
    pallas_call x0 -> x5, Pallas kernels: none -> 186 us  [the longest x1 56.2 us: all_gather(): pl.pallas_call(functools.partial(ag_kernel, nz), out_shape=jax.ShapeDtype...]
    psum x1 -> x0, blocking collectives: 143 us -> none  [shards(): squares = lax.psum(jnp.sum(right_part * right_part, axis=0), ('fsdp', 'tp'))]
    unnamed x1 -> x0, blocking collectives: 141 us -> none
    another operation x17 -> x0, other arithmetic: 124 us -> none  [the longest x14 83.6 us: shards(): lower = jnp.linalg.cholesky(gram)]
    unnamed x8 -> x0, starting transfers between devices: 27.7 us -> none
    dot_general x5 -> x0, matrix products: 24.8 us -> none  [the longest x1 6.97 us: shards(): jnp.dot(ortho, basis_block.T, precision=high, preferred_element_type=jnp....]
  transfers between devices with their start and end apart: 12 -> 0, of which waited for: 4 -> 0; matrix products, arithmetic and copies ran while one was open for 0% -> 0% of each run, Pallas kernels for 0% -> 0%
where the time goes in v2:
time: 192 us
  Pallas kernels  186 us (97%)
  local copies, waits for them, and re-layouts  5.07 us (3%)
    pallas_call x1, Pallas kernels, all_gather(): pl.pallas_call(functools.partial(ag_kernel, nz), out_shape=jax.ShapeDtype...  56.2 us
    pallas_call x1, Pallas kernels, scatter_and_gram(): pl.pallas_call(functools.partial(rs_kernel, nz, nt), out_shape=(jax.Shape...  47.5 us
    pallas_call x1, Pallas kernels, gather_and_factor(): pl.pallas_call(functools.partial(ag_chol_kernel, nz), out_shape=(jax.Shap...  42.1 us
    pallas_call x1, Pallas kernels, outputs(): pl.pallas_call(functools.partial(last_kernel, nt, factor), out_shape=(jax...  22.1 us
    pallas_call x1, Pallas kernels, left_sum(): pl.pallas_call(functools.partial(left_kernel, nt), out_shape=jax.ShapeDty...  18 us
    unnamed x9, local copies, waits for them, and re-layouts  4.12 us

profile of v2, /device:TPU:1, one launch (start us, length us, event | category | flops | bytes accessed | tf_op | source)
XLA Modules:
  0.0 191.8 jit_solution(1787661452588975791)
XLA Ops:
  0.6 0.0 copy-start.1
  0.6 0.0 copy-start
  0.7 0.9 reshape.18.own_ref
  1.6 56.2 %shard_map.58 = f32[16,4,112,128]{3,2,1,0:T(8,128)S(1)} custom-call(f32[112,128]{1,0:T(8,128)S(1)} %reshape.18.own_ref), custom_call_target="tpu_custom_call" | custom-call | tf_op jit(solution)/shard_map/pallas_call | solution.py:171
  57.8 0.0 copy-done.1
  57.9 0.0 copy-done
  57.9 18.0 %shard_map.59.l_ref = f32[128,512]{1,0:T(8,128)S(1)} custom-call(f32[128,1792]{1,0:T(8,128)S(1)} %copy-done, bf16[128,1792]{1,0:T(8,128)(2,1)S(1)} %copy-done.1, f32[7168,128]{1,0:T(8,128)S(1)} %bitcast.3), custom_call_target="tpu_custom_call" | custom-call | tf_op jit(solution)/shard_map/pallas_call | solution.py:451
  75.9 47.5 %shard_map.60 = (f32[112,128]{1,0:T(8,128)S(1)}, f32[8,4,64,128]{3,2,1,0:T(8,128)S(1)}) custom-call(f32[128,1792]{1,0:T(8,128)S(1)} %copy-done, bf16[128,1792]{1,0:T(8,128)(2,1)S(1)} %copy-done.1, f32[128,512]{1,0:T(8,128)S(1)} %shard_map.59.l_ref), custom_call_target="tpu_custom_call" | custom-call | tf_op jit(solution)/shard_map/pallas_call | solution.py:386
  123.4 42.1 %shard_map.61 = (f32[16,4,112,128]{3,2,1,0:T(8,128)S(1)}, f32[512,512]{1,0:T(8,128)S(1)}) custom-call(f32[112,128]{1,0:T(8,128)S(1)} %get-tuple-element.7.own_ref, f32[2048,128]{1,0:T(8,128)S(1)} %bitcast.5), custom_call_target="tpu_custom_call" | custom-call | tf_op jit(solution)/shard_map/pallas_call | solution.py:217
  165.6 0.0 copy-start.2
  165.6 1.8 copy-done.2
  167.4 22.1 %shard_map.62 = (f32[128,1792]{1,0:T(8,128)S(1)}, f32[28,512]{1,0:T(8,128)S(1)}, bf16[128,1792]{1,0:T(8,128)(2,1)S(1)}) custom-call(f32[128,1792]{1,0:T(8,128)S(1)} %copy-done, bf16[128,1792]{1,0:T(8,128)(2,1)S(1)} %copy-done.1, f32[128,512]{1,0:T(8,128)S(1)} %shard_map.59.l_ref, f32[512,512]{1,0:T(8,128)S(1)} %get-tuple-element.9.x_ref, ...), custom_call_target="tpu_custom_call" | custom-call | tf_op jit(solution)/shard_map/pallas_call | solution.py:700
  189.5 0.9 copy.9
  190.4 0.6 copy.10
  191.0 0.8 copy.11
Async XLA Ops:
  0.6 57.2 %copy-start.1 = (bf16[128,1792]{1,0:T(8,128)(2,1)S(1)}, bf16[128,1792]{1,0:T(8,128)(2,1)}, u32[]{:S(2)}) copy-start(bf16[128,1792]{1,0:T(8,128)(2,1)} %g_ref.5) | copy-start | bytes 1376260
  0.6 57.2 %copy-start = (f32[128,1792]{1,0:T(8,128)S(1)}, f32[128,1792]{1,0:T(8,128)}, u32[]{:S(2)}) copy-start(f32[128,1792]{1,0:T(8,128)} %m_ref.5) | copy-start | bytes 2752516
  165.6 1.8 copy-start.2

commit v3 on v2

--- a/solution.py
+++ b/solution.py
@@ -152,81 +152,6 @@
             if o:
                 self.zc(o).wait_send()
         self.zc(-8).wait_send()
-
-
-def ag_kernel(nz, own_ref, out_ref, *sems):
-    place = Place(nz)
-    out_ref[place.z, place.x] = own_ref[...]
-    greet(place.near())
-    gather = Gather(place, out_ref, sems)
-    gather.begin()
-    for todo in gather.events():
-        for f in todo:
-            f()
-    gather.finish()
-
-
-def all_gather(own, nz, cid):
-    c = own.shape[0]
-    return pl.pallas_call(
-        functools.partial(ag_kernel, nz),
-        out_shape=jax.ShapeDtypeStruct((nz, NX, c, LANE), F32),
-        in_specs=[VMEM],
-        out_specs=VMEM,
-        scratch_shapes=ag_sems(),
-        compiler_params=pltpu.CompilerParams(
-            collective_id=cid, has_side_effects=True, vmem_limit_bytes=48 << 20
-        ),
-    )(own)
-
-
-def ag_chol_kernel(nz, own_ref, g_ref, out_ref, x_ref, zz, *sems):
-    place = Place(nz)
-    out_ref[place.z, place.x] = own_ref[...]
-    greet(place.near())
-    gather = Gather(place, out_ref, sems)
-    gather.begin()
-    chol_init(zz, g_ref)
-    events = gather.events()
-    blocks = LANE // BLOCK
-
-    def between(p, s):
-        for pp in range(RANK // LANE):
-            at = pp * blocks + s
-            if at % 2 == 1 and at // 2 < len(events):
-
-                @pl.when(p == pp)
-                def _(at=at):
-                    for f in events[at // 2]:
-                        f()
-
-    def body(p, _):
-        chol_panel(zz, p, between)
-        return _
-
-    lax.fori_loop(0, RANK // LANE, body, 0)
-    for todo in events[RANK // BLOCK // 2 :]:
-        for f in todo:
-            f()
-    x_ref[...] = zz[:, RANK:]
-    gather.finish()
-
-
-def gather_and_factor(own, gram, nz, cid):
-    c = own.shape[0]
-    return pl.pallas_call(
-        functools.partial(ag_chol_kernel, nz),
-        out_shape=(
-            jax.ShapeDtypeStruct((nz, NX, c, LANE), F32),
-            jax.ShapeDtypeStruct((RANK, RANK), F32),
-        ),
-        in_specs=[VMEM] * 2,
-        out_specs=(VMEM,) * 2,
-        scratch_shapes=[pltpu.VMEM((RANK, 2 * RANK), F32)] + ag_sems(),
-        compiler_params=pltpu.CompilerParams(
-            collective_id=cid, has_side_effects=True, vmem_limit_bytes=48 << 20
-        ),
-    )(own, gram)
 
 
 def rs_scratch(c):
@@ -344,6 +269,22 @@
         self.zc(-8).wait_send()
 
 
+def rows_of(flat, at, n):
+    return jnp.concatenate(
+        [flat[pl.ds(at * NX + c, n, stride=NX), :] for c in range(RANK // LANE)], axis=1
+    )
+
+
+def to_flat(chunks, flat):
+    c = chunks.shape[2]
+
+    def body(i, _):
+        flat[pl.ds(pl.multiple_of(i * c, 8), c), :] = chunks[i // NX, lax.rem(i, NX)]
+        return _
+
+    lax.fori_loop(0, chunks.shape[0] * NX, body, 0)
+
+
 def w_rows(b_ref, l_ref, flat, cols):
     lh, ll = split2(l_ref[...])
     for j in range(0, cols, 256):
@@ -360,108 +301,57 @@
     lax.fori_loop(0, part.shape[0] * NX, body, 0)
 
 
-def rs_kernel(nz, nt, m_ref, g_ref, l_ref, out_ref, gram_ref, blend, flat, part, *scratch):
-    place = Place(nz)
-    cols = m_ref.shape[1]
-    n_rs = len(rs_scratch(8))
-    gram = Gram(place, nt, gram_ref, scratch[n_rs:])
-    gram.compute(l_ref)
-    zs = [place.dev(d, 0) for d in range(1, nz)]
-    xs = [place.dev(0, d) for d in range(1, NX)]
-    greet(zs + xs + [gram.peer(o) for o in range(1, nt)])
-    gram.stage1()
-    blend[...] = m_ref[...] + g_ref[...].astype(F32)
-    w_rows(blend, l_ref, flat, cols)
-    to_chunks(flat, part, out_ref.shape[0])
-    gram.stage2()
-    others = {3: gram.stage3, 6: gram.stage4, 9: gram.stage5}
-    Scatter(place, part, scratch[:n_rs]).run(out_ref, others)
-    gram.finish()
-
-
-def scatter_and_gram(momentum, gradient, left, nz, nt, cid):
-    rows, cols = momentum.shape
-    c = cols * RANK // LANE // (nz * NX)
-    n = RANK // nt // NX
-    return pl.pallas_call(
-        functools.partial(rs_kernel, nz, nt),
-        out_shape=(
-            jax.ShapeDtypeStruct((c, LANE), F32),
-            jax.ShapeDtypeStruct((nt, NX, n * RANK // LANE, LANE), F32),
-        ),
-        in_specs=[VMEM] * 3,
-        out_specs=(VMEM,) * 2,
-        scratch_shapes=[
-            pltpu.VMEM((rows, cols), F32),
-            pltpu.VMEM((cols * RANK // LANE, LANE), F32),
-            pltpu.VMEM((nz, NX, c, LANE), F32),
-        ] + rs_scratch(c) + gram_scratch(nz, nt),
-        compiler_params=pltpu.CompilerParams(
-            collective_id=cid, has_side_effects=True, vmem_limit_bytes=48 << 20
-        ),
-    )(momentum, gradient, left)
-
-
-def left_kernel(nt, m_ref, g_ref, q_ref, out_ref, part, land, s1, r1, s2, r2):
-    t = lax.axis_index("tp")
-    rows, cols = m_ref.shape
-    n = rows // nt
-    acc = None
-    for j in range(0, cols, 256):
-        b = split2(m_ref[:, j : j + 256] + g_ref[:, j : j + 256].astype(F32))
-        q = jnp.concatenate(
-            [q_ref[pl.ds(j * NX + c, 256, stride=NX), :] for c in range(RANK // LANE)], axis=1
-        )
-        d = dot3(b, q, NN)
-        acc = d if acc is None else acc + d
-    part[...] = acc
-
-    def peer(o):
-        return lax.rem(t + o, nt)
-
-    greet([{"tp": peer(o)} for o in range(1, nt)])
-
-    def piece(i):
-        return pl.ds(pl.multiple_of(i * n, n), n)
-
-    def out1(o):
-        return copy_to(part.at[piece(peer(o)), :], land.at[o], s1.at[o], r1.at[o], {"tp": peer(o)})
-
-    def out2(o):
-        ref = out_ref.at[piece(t), :]
-        return copy_to(ref, ref, s2.at[o], r2.at[o], {"tp": peer(o)})
-
-    for o in range(1, nt):
-        out1(o).start()
-    total = part[piece(t), :]
-    for o in range(1, nt):
-        out1(o).wait_recv()
-        total = total + land[o]
-    out_ref[piece(t), :] = total
-    for o in range(1, nt):
-        out2(o).start()
-    for o in range(1, nt):
-        out2(o).wait()
-        out1(o).wait_send()
-
-
-def left_sum(momentum, gradient, q, nt, cid):
-    rows = momentum.shape[0]
+def left_scratch(rows, nt):
     dma = pltpu.SemaphoreType.DMA
-    return pl.pallas_call(
-        functools.partial(left_kernel, nt),
-        out_shape=jax.ShapeDtypeStruct((rows, RANK), F32),
-        in_specs=[VMEM] * 3,
-        out_specs=VMEM,
-        scratch_shapes=[
-            pltpu.VMEM((rows, RANK), F32),
-            pltpu.VMEM((nt, rows // nt, RANK), F32),
-            dma((nt,)), dma((nt,)), dma((nt,)), dma((nt,)),
-        ],
-        compiler_params=pltpu.CompilerParams(
-            collective_id=cid, has_side_effects=True, vmem_limit_bytes=48 << 20
-        ),
-    )(momentum, gradient, q)
+    return [pltpu.VMEM((rows, RANK), F32), pltpu.VMEM((nt, rows // nt, RANK), F32)] + [dma((nt,))] * 4
+
+
+class Left:
+    def __init__(self, nt, out, scratch):
+        self.nt, self.out = nt, out
+        self.t = lax.axis_index("tp")
+        self.part, self.land, self.s1, self.r1, self.s2, self.r2 = scratch
+        self.n = out.shape[0] // nt
+
+    def peer(self, o):
+        return lax.rem(self.t + o, self.nt)
+
+    def piece(self, i):
+        return pl.ds(pl.multiple_of(i * self.n, self.n), self.n)
+
+    def out1(self, o):
+        to = self.peer(o)
+        return copy_to(self.part.at[self.piece(to), :], self.land.at[o],
+                       self.s1.at[o], self.r1.at[o], {"tp": to})
+
+    def out2(self, o):
+        ref = self.out.at[self.piece(self.t), :]
+        return copy_to(ref, ref, self.s2.at[o], self.r2.at[o], {"tp": self.peer(o)})
+
+    def compute(self, blend, flat):
+        acc = None
+        for j in range(0, blend.shape[1], 256):
+            d = dot3(blend[:, j : j + 256], rows_of(flat, j, 256), NN)
+            acc = d if acc is None else acc + d
+        self.part[...] = acc
+
+    def run(self):
+        for o in range(1, self.nt):
+            self.out1(o).start()
+        total = self.part[self.piece(self.t), :]
+        for o in range(1, self.nt):
+            self.out1(o).wait_recv()
+            total = total + self.land[o]
+        self.out[self.piece(self.t), :] = total
+        for o in range(1, self.nt):
+            self.out2(o).start()
+        for o in range(1, self.nt):
+            self.out2(o).wait_recv()
+
+    def finish(self):
+        for o in range(1, self.nt):
+            self.out1(o).wait_send()
+            self.out2(o).wait_send()
 
 
 def gram_scratch(nz, nt):
@@ -645,87 +535,175 @@
     zz[:, RANK:] = jnp.where(i == j, 1.0, 0.0).astype(F32)
 
 
-def last_kernel(nt, factor, m_ref, g_ref, l_ref, x_ref, own_ref, w_ref,
-                nm_ref, nb_ref, up_ref, wh, wl, sq, land, ss, rs):
+def last(nt, factor, m_ref, blend, left, x, own, flat, nm_ref, nb_ref, up_ref, scratch):
+    wh, wl, sq, land, ss, rs = scratch
     t = lax.axis_index("tp")
-    rows, cols = m_ref.shape
-    x = split2(x_ref[...])
+    cols = blend.shape[1]
+    x = split2(x)
     total = jnp.zeros((8, RANK), F32)
     for j in range(0, cols, 256):
-        w = jnp.concatenate(
-            [w_ref[pl.ds(j * NX + c, 256, stride=NX), :] for c in range(RANK // LANE)], axis=1
-        )
-        h, l = split2(w)
+        h, l = split2(rows_of(flat, j, 256))
         wh[j : j + 256, :] = h
         wl[j : j + 256, :] = l
         r = dot3((h, l), x, NT)
         total = total + jnp.sum((r * r).reshape(32, 8, RANK), axis=0)
     sq[...] = total
 
-    def peer(o):
-        return {"tp": lax.rem(t + o, nt)}
-
-    greet([peer(o) for o in range(1, nt)])
-
     def send(o):
-        return copy_to(sq, land.at[o], ss.at[o], rs.at[o], peer(o))
+        return copy_to(sq, land.at[o], ss.at[o], rs.at[o], {"tp": lax.rem(t + o, nt)})
 
     for o in range(1, nt):
         send(o).start()
-    ortho = dot3(l_ref[...], x, NT)
-    m1 = dot3(ortho, x, NN)
-    n_own = own_ref.shape[0] // NX
-    own = jnp.concatenate(
-        [own_ref[pl.ds(c, n_own, stride=NX), :] for c in range(RANK // LANE)], axis=1
-    )
-    right = dot3(own, x, NT)
+    ortho = dot3(left, x, NT)
+    m1 = split2(dot3(ortho, x, NN) * 0.1)
+    right = dot3(rows_of(own, 0, own.shape[0] // NX), x, NT)
+    for j in range(0, cols, 256):
+        w = (wh[j : j + 256, :], wl[j : j + 256, :])
+        nm_ref[:, j : j + 256] = blend[:, j : j + 256] - dot3(m1, w, NT)
     for o in range(1, nt):
         send(o).wait()
         total = total + land[o]
     inv = 1.0 / (jnp.sqrt(jnp.sum(total, axis=0, keepdims=True)) + 1e-06)
     nb_ref[...] = right * inv
     m2 = split2(dot3(ortho * (inv * factor), x, NN))
-    m1 = split2(m1 * 0.1)
     for j in range(0, cols, 256):
         w = (wh[j : j + 256, :], wl[j : j + 256, :])
-        nm_ref[:, j : j + 256] = (
-            m_ref[:, j : j + 256] + g_ref[:, j : j + 256].astype(F32) - dot3(m1, w, NT)
-        )
         up_ref[:, j : j + 256] = dot3(m2, w, NT).astype(BF16)
 
 
-def outputs(momentum, gradient, left, x, own, w, nt, factor, cid):
+def last_scratch(cols, nt):
+    dma = pltpu.SemaphoreType.DMA
+    return [
+        pltpu.VMEM((cols, RANK), BF16),
+        pltpu.VMEM((cols, RANK), BF16),
+        pltpu.VMEM((8, RANK), F32),
+        pltpu.VMEM((nt, 8, RANK), F32),
+        dma((nt,)), dma((nt,)),
+    ]
+
+
+def step_kernel(nz, nt, factor, m_ref, g_ref, q_ref, nm_ref, nb_ref, up_ref,
+                blend, chunks, chunks2, flat, part, own, left_ref, gram_ref, zz, *scratch):
+    scratch = list(scratch)
+
+    def take(like):
+        got = scratch[: len(like)]
+        del scratch[: len(like)]
+        return got
+
+    rows, cols = m_ref.shape
+    c = own.shape[0]
+    place = Place(nz)
+    gather = Gather(place, chunks, take(ag_sems()))
+    left = Left(nt, left_ref, take(left_scratch(rows, nt)))
+    gram = Gram(place, nt, gram_ref, take(gram_scratch(nz, nt)))
+    scatter = Scatter(place, part, take(rs_scratch(c)))
+    gather2 = Gather(place, chunks2, take(ag_sems()))
+    lasts = take(last_scratch(cols, nt))
+
+    for i in range(RANK // LANE):
+        own[pl.ds(i, c // NX, stride=NX), :] = q_ref[:, i * LANE : (i + 1) * LANE]
+    chunks[place.z, place.x] = own[...]
+    greet(
+        [place.dev(d, 0) for d in range(1, nz)]
+        + [place.dev(0, d) for d in range(1, NX)]
+        + [gram.peer(o) for o in range(1, nt)]
+    )
+    gather.begin()
+    blend[...] = m_ref[...] + g_ref[...].astype(F32)
+    for todo in gather.events():
+        for f in todo:
+            f()
+    gather.finish()
+
+    to_flat(chunks, flat)
+    left.compute(blend, flat)
+    left.run()
+    gram.compute(left_ref)
+    gram.stage1()
+    left.finish()
+    w_rows(blend, left_ref, flat, cols)
+    to_chunks(flat, part, c)
+    gram.stage2()
+    scatter.run(own, {3: gram.stage3, 6: gram.stage4, 9: gram.stage5})
+    chunks2[place.z, place.x] = own[...]
+    gather2.begin()
+    gram.finish()
+
+    flat_gram(gram_ref, flat)
+    chol_init(zz, flat)
+    events = gather2.events()
+    blocks = LANE // BLOCK
+
+    def between(p, s):
+        for pp in range(RANK // LANE):
+            at = pp * blocks + s
+            if at % 2 == 1 and at // 2 < len(events):
+
+                @pl.when(p == pp)
+                def _(at=at):
+                    for f in events[at // 2]:
+                        f()
+
+    def body(p, _):
+        chol_panel(zz, p, between)
+        return _
+
+    lax.fori_loop(0, RANK // LANE, body, 0)
+    for todo in events[RANK // BLOCK // 2 :]:
+        for f in todo:
+            f()
+    gather2.finish()
+    to_flat(chunks2, flat)
+    last(nt, factor, m_ref, blend, left_ref[...], zz[:, RANK:], own, flat,
+         nm_ref, nb_ref, up_ref, lasts)
+
+
+def flat_gram(gram_ref, flat):
+    n = gram_ref.shape[2]
+
+    def body(i, _):
+        flat[pl.ds(pl.multiple_of(i * n, 8), n), :] = gram_ref[i // NX, lax.rem(i, NX)]
+        return _
+
+    lax.fori_loop(0, gram_ref.shape[0] * NX, body, 0)
+
+
+def shards(nz, nt, factor, momentum, gradient, right_basis):
     rows, cols = momentum.shape
-    dma = pltpu.SemaphoreType.DMA
+    n_own = right_basis.shape[0]
+    c = n_own * RANK // LANE
+    n = RANK // nt // NX
     return pl.pallas_call(
-        functools.partial(last_kernel, nt, factor),
+        functools.partial(step_kernel, nz, nt, factor),
         out_shape=(
             jax.ShapeDtypeStruct((rows, cols), F32),
-            jax.ShapeDtypeStruct((own.shape[0] // NX, RANK), F32),
+            jax.ShapeDtypeStruct((n_own, RANK), F32),
             jax.ShapeDtypeStruct((rows, cols), BF16),
         ),
-        in_specs=[VMEM] * 6,
+        in_specs=[VMEM] * 3,
         out_specs=(VMEM,) * 3,
         scratch_shapes=[
-            pltpu.VMEM((cols, RANK), BF16),
-            pltpu.VMEM((cols, RANK), BF16),
-            pltpu.VMEM((8, RANK), F32),
-            pltpu.VMEM((nt, 8, RANK), F32),
-            dma((nt,)), dma((nt,)),
-        ],
+            pltpu.VMEM((rows, cols), F32),
+            pltpu.VMEM((nz, NX, c, LANE), F32),
+            pltpu.VMEM((nz, NX, c, LANE), F32),
+            pltpu.VMEM((cols * RANK // LANE, LANE), F32),
+            pltpu.VMEM((nz, NX, c, LANE), F32),
+            pltpu.VMEM((c, LANE), F32),
+            pltpu.VMEM((rows, RANK), F32),
+            pltpu.VMEM((nt, NX, n * RANK // LANE, LANE), F32),
+            pltpu.VMEM((RANK, 2 * RANK), F32),
+        ]
+        + ag_sems()
+        + left_scratch(rows, nt)
+        + gram_scratch(nz, nt)
+        + rs_scratch(c)
+        + ag_sems()
+        + last_scratch(cols, nt),
         compiler_params=pltpu.CompilerParams(
-            collective_id=cid, has_side_effects=True, vmem_limit_bytes=48 << 20
+            collective_id=1, has_side_effects=True, vmem_limit_bytes=56 << 20
         ),
-    )(momentum, gradient, left, x, own, w)
-
-
-def shards(nz, nt, factor, momentum, gradient, right_basis):
-    cols = momentum.shape[1]
-    q = all_gather(right_basis.reshape(-1, LANE), nz, 1)
-    left = left_sum(momentum, gradient, q.reshape(-1, LANE), nt, 2)
-    own, gram = scatter_and_gram(momentum, gradient, left, nz, nt, 3)
-    w, x = gather_and_factor(own, gram.reshape(-1, LANE), nz, 4)
-    return outputs(momentum, gradient, left, x, own, w.reshape(-1, LANE), nt, factor, 5)
+    )(momentum, gradient, right_basis)
 
 
 def solution(mesh):

time: 192 us -> 178 us (0.927)
  Pallas kernels: 186 us -> 174 us
    pallas_call x5 -> x1, Pallas kernels: 186 us -> 174 us  [shards(): pl.pallas_call(functools.partial(step_kernel, nz, nt, factor), out_shape=...]
    unnamed x9 -> x7, local copies, waits for them, and re-layouts: 4.12 us -> 3.62 us
where the time goes in v3:
time: 178 us
  Pallas kernels  174 us (98%)
  local copies, waits for them, and re-layouts  3.62 us (2%)
    pallas_call x1, Pallas kernels, shards(): pl.pallas_call(functools.partial(step_kernel, nz, nt, factor), out_shape=...  174 us
    unnamed x7, local copies, waits for them, and re-layouts  3.62 us

profile of v3, /device:TPU:1, one launch (start us, length us, event | category | flops | bytes accessed | tf_op | source)
XLA Modules:
  0.0 177.8 jit_solution(2665956601717987973)
XLA Ops:
  0.6 173.5 %shard_map.58 = (f32[128,1792]{1,0:T(8,128)}, f32[28,512]{1,0:T(8,128)}, bf16[128,1792]{1,0:T(8,128)(2,1)}) custom-call(f32[128,1792]{1,0:T(8,128)} %m_ref.1, bf16[128,1792]{1,0:T(8,128)(2,1)} %g_ref.1, f32[28,512]{1,0:T(8,128)} %q_ref.1), custom_call_target="tpu_custom_call" | custom-call | tf_op jit(solution)/shard_map/pallas_call | solution.py:677
  174.1 0.0 copy-start.1
  174.2 0.0 copy-start
  174.2 2.2 %copy.9 = f32[128,1792]{1,0:T(8,128)} copy(f32[128,1792]{1,0:T(8,128)} %get-tuple-element.6) | data formatting | bytes 1835008
  176.4 0.0 copy-done.1
  176.4 0.6 copy.10
  177.0 0.0 copy-done
  177.0 0.8 copy.11
Async XLA Ops:
  174.1 2.2 %copy-start.1 = (f32[28,512]{1,0:T(8,128)S(1)}, f32[28,512]{1,0:T(8,128)}, u32[]{:S(2)}) copy-start(f32[28,512]{1,0:T(8,128)} %get-tuple-element.7) | copy-start | bytes 172036
  174.2 2.9 %copy-start = (bf16[128,1792]{1,0:T(8,128)(2,1)S(1)}, bf16[128,1792]{1,0:T(8,128)(2,1)}, u32[]{:S(2)}) copy-start(bf16[128,1792]{1,0:T(8,128)(2,1)} %get-tuple-element.8) | copy-start | bytes 1376260
